TPU v7x, 32 devices: a whole 2x2x4 slice. The times are simulated.
32 devices in a mesh: spot: 8 (over y, x, core), gene: 4 (over z).
Axes of the slice: x: 2, y: 2, z: 4, core: 2. Of those that a mesh axis runs over, the one named last changes fastest.
Arguments:
- counts: int32 [32, 512, 4096], P('spot', None, 'gene'), may hold values from 0 to 56, as said below
- tissue: int32 [32, 512], P('spot'), may hold values from 0 to 1
- tile_ids: int32 [32, 512], P('spot'), may hold values from 0 to 16383, as said below
Outputs:
- statistic: float32 [4096, 4096], P('gene', 'spot')
Inputs may be any that keep to these rules, and one draw needn't show every extreme that they name: `counts`: whole numbers of molecules. `tile_ids`: bins of one tile form a rectangle of the grid; tiles are bands of rows crossed with bands of columns.
All inputs are finite; a program needn't handle non-finite values.
Results may differ from a plain program's by a relative error of at most 0.003.
Values may be sent and summed in bfloat16 or wider, within the bound.
A program may use at most 128 MiB of HBM per device.

v0:
```python
import jax
import jax.numpy as jnp
from jax import lax
from jax.sharding import PartitionSpec as P

stencil_taps = [
    (row_off, col_off, 1.0 / (row_off * row_off + col_off * col_off))
    for row_off in range(-2, 3)
    for col_off in range(-2, 3)
    if row_off != 0 or col_off != 0
]
contract_bins = (((0,), (0,)), ((), ()))


def padded(cells, sides, width):
    for axis, dim in sides:
        count = lax.axis_size(axis)
        ends = count - 1
        head = lax.slice_in_dim(cells, 0, width, axis=dim)
        tail = lax.slice_in_dim(cells, cells.shape[dim] - width, cells.shape[dim], axis=dim)
        cells = jnp.concatenate(
            [
                lax.ppermute(tail, axis, [(i, (i + 1) % count) for i in range(ends)]),
                cells,
                lax.ppermute(head, axis, [((i + 1) % count, i) for i in range(ends)]),
            ],
            axis=dim,
        )
    return cells


def cross_panel(left, right):
    return lax.dot_general(left, right, contract_bins, preferred_element_type=jnp.float32)


def shards(counts, tissue, tile_ids):
    row_count, col_count, panel_width = counts.shape
    tile_code = tile_ids * 2 + tissue
    code_rims = padded(tile_code, (("spot", 0),), 2)
    code_wide = jnp.pad(code_rims, ((0, 0), (2, 2)))
    tissue_wide = (code_wide % 2).astype(jnp.float32)
    ids_wide = code_wide // 2
    in_tissue = tissue.astype(jnp.float32)
    weight_sq = jnp.zeros((row_count, col_count), jnp.float32)
    same_list = []
    for row_off, col_off, weight in stencil_taps:
        near_ids = ids_wide[
            2 + row_off : 2 + row_off + row_count, 2 + col_off : 2 + col_off + col_count
        ]
        near_tissue = tissue_wide[
            2 + row_off : 2 + row_off + row_count, 2 + col_off : 2 + col_off + col_count
        ]
        same_tile = (near_ids == tile_ids).astype(jnp.float32)
        weight_sq = weight_sq + weight * weight * same_tile * near_tissue
        same_list.append(same_tile)
    pair_local = jnp.sum(in_tissue * weight_sq)
    count_local = jnp.sum(in_tissue)
    values = counts.astype(jnp.float32)
    masked = values * in_tissue[:, :, None]
    first_sums = jnp.sum(masked, axis=(0, 1))
    total_first, tissue_count, pair_norm = lax.psum((first_sums, count_local, pair_local), "spot")
    gene_mean = total_first / tissue_count
    centred = (values - gene_mean) * in_tissue[:, :, None]
    variance = lax.psum(jnp.sum(centred * centred, axis=(0, 1)), "spot") / tissue_count
    zscores = (centred / jnp.sqrt(variance + 1e-05)).astype(jnp.bfloat16)
    zscore_rims = padded(zscores, (("spot", 0),), 2)
    zscore_wide = jnp.pad(zscore_rims, ((0, 0), (2, 2), (0, 0)))
    lagged_sum = jnp.zeros(values.shape, jnp.float32)
    for (row_off, col_off, weight), same_tile in zip(stencil_taps, same_list):
        near_z = zscore_wide[
            2 + row_off : 2 + row_off + row_count, 2 + col_off : 2 + col_off + col_count, :
        ]
        lagged_sum = lagged_sum + weight * same_tile[:, :, None] * near_z.astype(jnp.float32)
    lagged = lagged_sum.astype(jnp.bfloat16)
    bin_count = row_count * col_count
    flat_z = zscores.reshape(bin_count, panel_width)
    flat_lag = lagged.reshape(bin_count, panel_width)
    totals = cross_panel(flat_z, lax.all_gather(flat_lag, "gene", axis=1, tiled=True))
    share = lax.psum_scatter(totals, "spot", scatter_dimension=1, tiled=True)
    return share / jnp.sqrt(pair_norm)


def solution(mesh):
    placed = (P("spot", None, "gene"), P("spot", None), P("spot", None))
    return jax.shard_map(
        shards, mesh=mesh, in_specs=placed, out_specs=P("gene", "spot"), check_vma=False
    )
```

profile of v0, /device:TPU:3, one launch (start us, length us, event | category | flops | bytes accessed | tf_op | source)
XLA Modules:
  0.0 599.2 jit_solution(11826082418916579114)
XLA Ops:
  6.5 0.8 multiply_add_fusion
  7.3 3.7 collective-permute-start
  11.0 1.9 collective-permute-start.1
  12.9 1.3 convert_reduce_fusion
  14.3 4.3 multiply_reduce_fusion.1
  18.6 12.2 %all-reduce.3 = (f32[1024]{0:T(1024)S(1)}, f32[]{:T(128)}) all-reduce(f32[1024]{0:T(1024)S(1)} %multiply_reduce_fusion.1, f32[]{:T(128)} %convert_reduce_fusion), channel_id=1, replica_groups=mesh['spot'=8,'gene'=4] {'spot'}, use_global_device_ids=true, to_apply=%region_1.2 | all-reduce | flops 1025 | bytes 8200 | tf_op jit(solution)/shard_map/psum | solution.py:61
  30.8 0.6 broadcast_divide_fusion.1
  31.4 4.2 multiply_reduce_fusion
  35.6 0.0 collective-permute-done
  35.6 0.0 collective-permute-done.1
  35.7 0.1 add_select_fusion.1
  35.8 0.1 broadcast_select_fusion.8
  35.9 0.1 fusion.37
  36.0 0.2 broadcast_select_fusion.19
  36.1 0.8 fusion.14
  36.9 12.7 %all-reduce.2 = (f32[1024]{0:T(1024)S(1)}, f32[]{:T(128)}) all-reduce(f32[1024]{0:T(1024)S(1)} %multiply_reduce_fusion, f32[]{:T(128)} %fusion.14), channel_id=1, replica_groups=mesh['spot'=8,'gene'=4] {'spot'}, use_global_device_ids=true, to_apply=%region_5.6 | all-reduce | flops 1025 | bytes 8200 | tf_op jit(solution)/shard_map/psum | solution.py:64
  49.6 0.7 add_sqrt_fusion
  50.3 4.1 divide_convert_fusion
  54.4 0.5 fusion.41
  54.9 5.1 collective-permute-start.2
  60.0 1.9 collective-permute-start.3
  62.0 42.8 %collective-permute-done.2 = bf16[2,512,1024]{2,1,0:T(8,128)(2,1)S(1)} collective-permute-done((bf16[2,512,1024]{2,1,0:T(8,128)(2,1)S(1)}, bf16[2,512,1024]{2,1,0:T(8,128)(2,1)S(1)}, u32[]{:S(2)}, u32[]{:S(2)}) %collective-permute-start.2) | collective-permute-done | bytes 2097184 | tf_op jit(solution)/shard_map/ppermute | solution.py:23
  104.8 0.5 collective-permute-done.3
  105.3 5.0 fusion.5
  110.3 52.5 %add_convert_fusion = bf16[4,512,1024]{2,1,0:T(8,128)(2,1)} fusion(bf16[4,512,1024]{2,1,0:T(8,128)(2,1)S(1)} %divide_convert_fusion, bf16[2,512,1024]{2,1,0:T(8,128)(2,1)} %copy-done.1, bf16[2,512,1024]{2,1,0:T(8,128)(2,1)S(1)} %collective-permute-done.2, bf16[8,516,1024]{2,1,0:T(8,128)(2,1)} %fusion.5, f32[4,512]{1,0:T(4,128)S(1)} %get-tuple-element.93, ...), kind=kLoop, calls=%fused_computation.8 | loop fusion | flops 159383552 | bytes 96665600 | tf_op jit(solution)/shard_map/convert_element_type | solution.py:74
  162.8 0.0 all-gather.2.cloned.1.call-update
  162.8 0.2 reduce-scatter.2.cloned.1.call-start
  163.1 288.4 %all-gather.2.cloned.1.call-done = bf16[2048,4096]{1,0:T(8,128)(2,1)} async-done(((bf16[2048,1024]{1,0:T(8,128)(2,1)}), bf16[2048,4096]{1,0:T(8,128)(2,1)}) %all-gather.2.cloned.1.call-update) | async-done | bytes 16777232 | tf_op jit(solution)/shard_map/all_gather | solution.py:78
  451.4 23.8 %fusion.43 = f32[1024,4096]{1,0:T(8,128)} fusion(bf16[2048,1024]{1,0:T(8,128)(2,1)} %bitcast.4, bf16[2048,4096]{1,0:T(8,128)(2,1)} %all-gather.2.cloned.1.call-done), kind=kOutput, calls=%fused_computation.137 | convolution fusion | flops 17179869184 | bytes 37748736 | tf_op jit(solution)/shard_map/dot_general | solution.py:33
  475.2 0.0 reduce-scatter.2.cloned.1.call-update
  475.9 113.4 %reduce-scatter.2.cloned.1.call-done = f32[1024,512]{1,0:T(8,128)} async-done(((f32[1024,4096]{1,0:T(8,128)}), f32[1024,512]{1,0:T(8,128)}) %reduce-scatter.2.cloned.1.call-update) | async-done | bytes 2097168 | tf_op jit(solution)/shard_map/reduce_scatter | solution.py:79
  589.2 3.1 broadcast_divide_fusion
  (11 shorter events, 0.0 us)
Async XLA Ops:
  6.5 444.9 %all-gather.2.cloned.1.call-start = ((), (), s32[]{:S(2)}) async-start(), calls=%async_computation.1 | async-start | bytes 20971520 | tf_op jit(solution)/shard_map/all_gather | solution.py:78
  7.3 28.3 %collective-permute-start = (s32[2,512]{1,0:T(2,128)S(1)}, s32[2,512]{1,0:T(2,128)S(1)}, u32[]{:S(2)}, u32[]{:S(2)}) collective-permute-start(s32[2,512]{1,0:T(2,128)S(1)} %get-tuple-element.103), channel_id=1, source_target_pairs={{0,4},{4,8},{8,12},{12,16},{16,20},{20,24},{24,28},{1,5},{5,9},{9,... | collective-permute-start | bytes 12296 | tf_op jit(solution)/shard_map/ppermute | solution.py:23
  11.0 24.6 %collective-permute-start.1 = (s32[2,512]{1,0:T(2,128)S(1)}, s32[2,512]{1,0:T(2,128)S(1)}, u32[]{:S(2)}, u32[]{:S(2)}) collective-permute-start(s32[2,512]{1,0:T(2,128)S(1)} %get-tuple-element.104), channel_id=1, source_target_pairs={{4,0},{8,4},{12,8},{16,12},{20,16},{24,20},{28,24},{5,1},{9,5},{13... | collective-permute-start | bytes 12296 | tf_op jit(solution)/shard_map/ppermute | solution.py:25
  14.2 21.5 %copy-start.2 = (s32[4,512]{1,0:T(4,128)S(1)}, s32[4,512]{1,0:T(4,128)}, u32[]{:S(2)}) copy-start(s32[4,512]{1,0:T(4,128)} %param.5) | copy-start | bytes 24580
  14.3 21.9 %copy-start.3 = (s32[4,512]{1,0:T(4,128)S(1)}, s32[4,512]{1,0:T(4,128)}, u32[]{:S(2)}) copy-start(s32[4,512]{1,0:T(4,128)} %param.4) | copy-start | bytes 24580
  54.4 55.9 %copy-start = (bf16[4,512,1024]{2,1,0:T(8,128)(2,1)}, bf16[4,512,1024]{2,1,0:T(8,128)(2,1)S(1)}, u32[]{:S(2)}) copy-start(bf16[4,512,1024]{2,1,0:T(8,128)(2,1)S(1)} %divide_convert_fusion) | copy-start | bytes 12582916
  54.9 49.9 %collective-permute-start.2 = (bf16[2,512,1024]{2,1,0:T(8,128)(2,1)S(1)}, bf16[2,512,1024]{2,1,0:T(8,128)(2,1)S(1)}, u32[]{:S(2)}, u32[]{:S(2)}) collective-permute-start(bf16[2,512,1024]{2,1,0:T(8,128)(2,1)S(1)} %get-tuple-element.57), channel_id=1, source_target_pairs={{0,4},{4,8},{8,12},{12,16},{16,20},{20,24},{24,28},{1,5},{5,9},{9,... | collective-permute-start | bytes 6291464 | tf_op jit(solution)/shard_map/ppermute | solution.py:23
  60.0 45.2 %collective-permute-start.3 = (bf16[2,512,1024]{2,1,0:T(8,128)(2,1)S(1)}, bf16[2,512,1024]{2,1,0:T(8,128)(2,1)S(1)}, u32[]{:S(2)}, u32[]{:S(2)}) collective-permute-start(bf16[2,512,1024]{2,1,0:T(8,128)(2,1)S(1)} %get-tuple-element.58), channel_id=1, source_target_pairs={{4,0},{8,4},{12,8},{16,12},{20,16},{24,20},{28,24},{5,1},{9,5},{13... | collective-permute-start | bytes 6291464 | tf_op jit(solution)/shard_map/ppermute | solution.py:25
  105.3 5.0 copy-start.1
  162.8 426.4 %reduce-scatter.2.cloned.1.call-start = ((), (), s32[]{:S(2)}) async-start(), calls=%async_computation.2 | async-start | bytes 18874368 | tf_op jit(solution)/shard_map/reduce_scatter | solution.py:79
Sparse Core Ops, SparseCore 0:
  162.9 288.4 all-gather.1
  475.4 113.7 reduce-scatter.1
where the time goes:
time: 601 us; the launch traced here: 599 us
  waiting for transfers between devices  445 us (74%)
  other arithmetic  77.8 us (13%)
  blocking collectives  25 us (4%)
  matrix products  23.8 us (4%)
  between operations  14.2 us (2%)
  starting transfers between devices  12.8 us (2%)
    all_gather x1, waiting for transfers between devices, shards(): lax.all_gather(flat_lag, 'gene', axis=1, tiled=True)  288 us
    reduce_scatter x1, waiting for transfers between devices, shards(): share = lax.psum_scatter(totals, 'spot', scatter_dimension=1, tiled=True)  113 us
    convert_element_type x1, other arithmetic, shards(): lagged = lagged_sum.astype(jnp.bfloat16)  52.5 us
    ppermute x2, waiting for transfers between devices, padded(): lax.ppermute(tail, axis, [(i, (i + 1) % count) for i in range(ends)])  42.8 us
    dot_general x1, matrix products, cross_panel(): lax.dot_general(left, right, contract_bins, preferred_element_type=jnp.fl...  23.8 us
    psum x1, blocking collectives, shards(): lax.psum(jnp.sum(centred * centred, axis=(0, 1)), 'spot') / tissue_count  12.7 us
    psum x1, blocking collectives, shards(): lax.psum((first_sums, count_local, pair_local), 'spot')  12.2 us
  transfers between devices with their start and end apart: 6, of which 4 were waited for; matrix products, arithmetic and copies ran while one was open for 2% of the time, Pallas kernels for 0%

commit v1 on v0

--- a/solution.py
+++ b/solution.py
@@ -1,6 +1,8 @@
 import jax
 import jax.numpy as jnp
 from jax import lax
+from jax.experimental import pallas as pl
+from jax.experimental.pallas import tpu as pltpu
 from jax.sharding import PartitionSpec as P
 
 stencil_taps = [
@@ -33,7 +35,7 @@
     return lax.dot_general(left, right, contract_bins, preferred_element_type=jnp.float32)
 
 
-def shards(counts, tissue, tile_ids):
+def plain_shards(counts, tissue, tile_ids):
     row_count, col_count, panel_width = counts.shape
     tile_code = tile_ids * 2 + tissue
     code_rims = padded(tile_code, (("spot", 0),), 2)
@@ -80,8 +82,229 @@
     return share / jnp.sqrt(pair_norm)
 
 
+weight_table = [
+    [0.0 if dr == 0 and dc == 0 else 40.0 / (dr * dr + dc * dc) for dc in range(3)]
+    for dr in range(3)
+]
+
+P_IN = [(0, 1), (3, 2)]
+P_CROSS = [(1, 2), (2, 1)]
+P_OUT = [(1, 0), (2, 3)]
+
+
+def lag_kernel(row_same, z_ref, mat_ref, lag_ref):
+    rows = lag_ref.shape[0]
+
+    @pl.loop(0, rows)
+    def _(r):
+        acc = jnp.dot(mat_ref[0], z_ref[r + 2], preferred_element_type=jnp.float32)
+        for step, mat in ((0, 2), (1, 1), (3, 1), (4, 2)):
+            part = jnp.dot(mat_ref[mat], z_ref[r + step], preferred_element_type=jnp.float32)
+            acc = acc + row_same[r, step] * part
+        lag_ref[r] = (acc * (1.0 / 40.0)).astype(lag_ref.dtype)
+
+
+def lag_call(row_same, z_wide, mats):
+    rows = z_wide.shape[0] - 4
+    cols, genes = z_wide.shape[1:]
+    tall = mats.shape[1]
+    return pl.pallas_call(
+        lag_kernel,
+        out_shape=jax.ShapeDtypeStruct((rows, tall, genes), jnp.bfloat16),
+        in_specs=[
+            pl.BlockSpec(memory_space=pltpu.SMEM),
+            pl.BlockSpec(memory_space=pltpu.VMEM),
+            pl.BlockSpec(memory_space=pltpu.VMEM),
+        ],
+        out_specs=pl.BlockSpec(memory_space=pltpu.VMEM),
+        compiler_params=pltpu.CompilerParams(vmem_limit_bytes=40 * 1024 * 1024),
+        cost_estimate=pl.CostEstimate(
+            flops=rows * 10 * tall * cols * genes, bytes_accessed=12 * 2**20, transcendentals=0
+        ),
+    )(row_same, z_wide, mats)
+
+
+def pair_sum(code_all, rows, cols):
+    code_wide = jnp.pad(code_all, 2)
+    tissue_wide = (code_wide % 2).astype(jnp.float32)
+    ids_wide = code_wide // 2
+    ids = code_all // 2
+    weight_sq = jnp.zeros((rows, cols), jnp.float32)
+    for row_off, col_off, weight in stencil_taps:
+        window = (slice(2 + row_off, 2 + row_off + rows), slice(2 + col_off, 2 + col_off + cols))
+        same_tile = (ids_wide[window] == ids).astype(jnp.float32)
+        weight_sq = weight_sq + weight * weight * same_tile * tissue_wide[window]
+    return jnp.sum((code_all % 2).astype(jnp.float32) * weight_sq)
+
+
+def mirrored_shards(counts, tissue, tile_ids):
+    rows, cols, width = counts.shape
+    half = width // 2
+    spots, genes = lax.axis_size("spot"), lax.axis_size("gene")
+    spot, g = lax.axis_index("spot"), lax.axis_index("gene")
+    core, chip = spot % 2, spot // 2
+    x, y = chip % 2, chip // 2
+    low, inner = g < 2, (g == 1) | (g == 2)
+    swap = lambda a, bit: lax.ppermute(a, "spot", [(i, i ^ bit) for i in range(spots)])
+    along = lambda a, perm: lax.ppermute(a, "gene", perm)
+    ordered = lambda flag, a, b, dim: jnp.where(
+        flag, jnp.concatenate([a, b], dim), jnp.concatenate([b, a], dim)
+    )
+
+    code = tile_ids * 2 + tissue
+    raw = (counts * tissue[:, :, None]).astype(jnp.bfloat16)
+    kept = lax.dynamic_slice_in_dim(raw, core * half, half, 2)
+    given = lax.dynamic_slice_in_dim(raw, (1 - core) * half, half, 2)
+    taken = swap(given, 1)
+    code_taken = swap(code, 1)
+    first = core == 0
+    both = ordered(first, kept, taken, 0)
+    code_both = ordered(first, code, code_taken, 0)
+    tissue_both = (code_both % 2).astype(jnp.float32)
+    bins_here = jnp.sum(tissue_both)
+    both_f = both.astype(jnp.float32)
+    shift = jnp.round(jnp.sum(both_f, axis=(0, 1)) / jnp.maximum(bins_here, 1.0))
+    dev_f = both_f - tissue_both[:, :, None] * shift
+    dev = dev_f.astype(jnp.bfloat16)
+
+    mid, edge = cols // 2, 16
+    part_a = jnp.where(low, dev[:, : mid + edge], dev[:, mid - edge :])
+    part_b = jnp.where(low, dev[:, mid + edge :], dev[:, : mid - edge])
+    pieces = [part_a[:rows], part_a[rows:]]
+    in_a = [along(p, P_IN) for p in pieces]
+    cross_a = [along(p, P_CROSS) for p in pieces]
+    out_inner = [along(p, P_OUT) for p in cross_a]
+    cross_outer = [along(p, P_CROSS) for p in in_a]
+    in_b = along(part_b, P_IN)
+    out_outer = [along(p, P_OUT) for p in cross_outer]
+
+    steps = spots - 2
+    above = lax.ppermute(dev[-2:], "spot", [(i, i + 2) for i in range(steps)])
+    below = lax.ppermute(dev[:2], "spot", [(i + 2, i) for i in range(steps)])
+
+    code_all = lax.all_gather(code, "spot", axis=0, tiled=True)
+    dev_back = dev.astype(jnp.float32)
+    local = jnp.stack(
+        [
+            jnp.sum(dev_back, axis=(0, 1)),
+            jnp.sum(dev_back * dev_back, axis=(0, 1)),
+            shift,
+            jnp.full((half,), bins_here),
+        ]
+    )
+    every = lax.all_gather(local, "spot", axis=0).reshape(spots // 2, 2, 4, half)
+    every = lax.dynamic_index_in_dim(every, core, 1, keepdims=False)
+    sum1, sum2, shifts, bins = every[:, 0], every[:, 1], every[:, 2], every[:, 3]
+    tissue_count = jnp.sum(bins, axis=0)
+    mean = jnp.sum(sum1 + bins * shifts, axis=0) / tissue_count
+    gap = mean - shifts
+    variance = jnp.sum(sum2 - 2.0 * gap * sum1 + bins * gap * gap, axis=0) / tissue_count
+    scale = 1.0 / jnp.sqrt(variance + 1e-05)
+    pair_norm = pair_sum(code_all, rows * spots, cols)
+
+    band = 2 * rows
+    code_pad = jnp.pad(code_all, ((2, 2), (0, 0)), constant_values=-2)
+    code_wide = lax.dynamic_slice_in_dim(code_pad, chip * band, band + 4, 0)
+    tissue_wide = (code_wide % 2).astype(jnp.float32)
+    gap_pad = jnp.pad(gap, ((1, 1), (0, 0)))
+    gap_near = lax.dynamic_slice_in_dim(gap_pad, chip, 3, 0)
+    gap_here = gap_near[1]
+    gap_rows = jnp.concatenate(
+        [
+            jnp.broadcast_to(gap_near[k], (count, half))
+            for k, count in ((0, 2), (1, band), (2, 2))
+        ]
+    )
+    wide = jnp.concatenate([above, dev, below]).astype(jnp.float32)
+    z_wide = (
+        (wide - tissue_wide[:, :, None] * gap_rows[:, None, :]) * scale
+    ).astype(jnp.bfloat16)
+
+    edge_ids = code_wide[:, 0] // 2
+    row_same = jnp.stack(
+        [(edge_ids[k : k + band] == edge_ids[2 : 2 + band]).astype(jnp.float32) for k in range(5)], 1
+    )
+    line = code_all[0] // 2
+    col_same = line[:, None] == line[None, :]
+    spread = jnp.abs(jnp.arange(cols)[:, None] - jnp.arange(cols)[None, :])
+    at = lax.broadcasted_iota(jnp.int32, (mid + edge, cols), 0) + jnp.where(low, mid - edge, 0)
+    across = (at >= mid) != (lax.broadcasted_iota(jnp.int32, (mid + edge, cols), 1) >= mid)
+    here = (at >= mid) == low
+    share = jnp.where(across, 0.5, jnp.where(here, 1.0, 0.0))
+    cut = lambda a: jnp.where(low, a[mid - edge :], a[: mid + edge])
+    mats = []
+    for table in weight_table:
+        mat = jnp.zeros((cols, cols), jnp.float32)
+        for dc, weight in enumerate(table):
+            mat = jnp.where(spread == dc, weight, mat)
+        mat = jnp.where(col_same, mat, 0.0)
+        mats.append(jnp.concatenate([mat, cut(mat) * share]).astype(jnp.bfloat16))
+    lag = lag_call(row_same, z_wide, jnp.stack(mats))
+    lag_taken = swap(lag, 1)
+    lag_both = ordered(first, lag, lag_taken, 2)
+    flat = lambda a: a.reshape(-1, a.shape[-1])
+    lag_all, lag_part = flat(lag_both[:, :cols]), flat(lag_both[:, cols:])
+    tissue_part = jnp.where(low, tissue_both[:, mid - edge :], tissue_both[:, : mid + edge])
+    lag_sum = lambda a, t: cross_panel(a, t.reshape(-1, 1).astype(jnp.bfloat16))
+    sum_all, sum_part = lag_sum(lag_all, tissue_both), lag_sum(lag_part, tissue_part)
+
+    panels = lax.all_gather(jnp.stack([gap_here, scale]), "gene", axis=0)
+    of_panel = lambda h: lax.dynamic_index_in_dim(panels, h, 0, keepdims=False)
+
+    def settle(product, total, h):
+        pair = of_panel(h)
+        return (product - total * pair[0]) * pair[1]
+
+    own = settle(cross_panel(lag_all, flat(dev)), sum_all, g)
+    near_panel = ordered(low, jnp.concatenate(in_a), in_b, 1)
+    near = settle(cross_panel(lag_all, flat(near_panel)), sum_all, g ^ 1)
+    near = jnp.where(inner, near, 0.0)
+    far_in = jnp.concatenate([jnp.where(inner, p, q) for p, q in zip(cross_a, out_inner)])
+    far_out = jnp.concatenate([jnp.where(inner, p, q) for p, q in zip(cross_outer, out_outer)])
+    far_in = settle(cross_panel(lag_part, flat(far_in)), sum_part, jnp.where(low, 2, 1))
+    far_out = settle(cross_panel(lag_part, flat(far_out)), sum_part, jnp.where(low, 3, 0))
+
+    even = g % 2 == 0
+    near_0, near_1 = jnp.where(even, own, near), jnp.where(even, near, own)
+    far_0, far_1 = jnp.where(low, far_in, far_out), jnp.where(low, far_out, far_in)
+    grid = [
+        [jnp.where(low, near_0, far_0), jnp.where(low, near_1, far_1)],
+        [jnp.where(low, far_0, near_0), jnp.where(low, far_1, near_1)],
+    ]
+    narrow = lambda a: a.astype(jnp.bfloat16)
+    widen = lambda a: a.astype(jnp.float32)
+
+    def fold(blocks, bits, places):
+        pairs = blocks
+        send = [narrow(jnp.where(places[0] == 0, pairs[1][k], pairs[0][k])) for k in range(2)]
+        keep = [jnp.where(places[0] == 0, pairs[0][k], pairs[1][k]) for k in range(2)]
+        keep = [a + widen(swap(b, bits[0])) for a, b in zip(keep, send)]
+        send = narrow(jnp.where(places[1] == 0, keep[1], keep[0]))
+        return jnp.where(places[1] == 0, keep[0], keep[1]) + widen(swap(send, bits[1]))
+
+    top = fold([[grid[i][j][:half] for j in range(2)] for i in range(2)], (4, 2), (y, x))
+    bottom = fold([[grid[j][i][half:] for j in range(2)] for i in range(2)], (2, 4), (x, y))
+
+    places = [(h, c, k) for h in range(genes) for c in range(2) for k in range(genes) if h != k]
+    where_is = lambda h, c, k: (2 * h + c) * genes + k
+    same_core = [(where_is(h, c, k), where_is(k, c, h)) for h, c, k in places]
+    other_core = [(where_is(h, c, k), where_is(k, 1 - c, h)) for h, c, k in places]
+    top_n, bottom_n = narrow(top), narrow(bottom)
+    got_same = lax.ppermute(jnp.where(first, top_n, bottom_n), ("spot", "gene"), same_core)
+    got_other = lax.ppermute(jnp.where(first, bottom_n, top_n), ("spot", "gene"), other_core)
+    norm = 1.0 / jnp.sqrt(pair_norm)
+    top = (top + widen(jnp.where(first, got_same, got_other)).T) * norm
+    bottom = (bottom + widen(jnp.where(first, got_other, got_same)).T) * norm
+    return jnp.concatenate([top, bottom])
+
+
 def solution(mesh):
     placed = (P("spot", None, "gene"), P("spot", None), P("spot", None))
+    fits = mesh.shape["gene"] == 4 and mesh.shape["spot"] == 8
     return jax.shard_map(
-        shards, mesh=mesh, in_specs=placed, out_specs=P("gene", "spot"), check_vma=False
-    )
+        mirrored_shards if fits else plain_shards,
+        mesh=mesh,
+        in_specs=placed,
+        out_specs=P("gene", "spot"),
+        check_vma=False,
+    )

time: 601 us -> 495 us (0.82)
  waiting for transfers between devices: 445 us -> 172 us
  blocking collectives: 25 us -> 92.4 us
  local copies, waits for them, and re-layouts: 0.5 us -> 40.9 us
  starting transfers between devices: 12.8 us -> 44.7 us
  matrix products: 23.8 us -> 45.9 us
  Pallas kernels: 0 us -> 21.3 us
  between operations: 14.2 us -> 2.12 us
  other arithmetic: 77.8 us -> 70.9 us
    all_gather x1 -> x0, waiting for transfers between devices: 288 us -> none  [shards(): lax.all_gather(flat_lag, 'gene', axis=1, tiled=True)]
    ppermute x4 -> x24, waiting for transfers between devices: 43.3 us -> 172 us  [the longest x11 54.5 us: mirrored_shards(): along = lambda a, perm: lax.ppermute(a, 'gene', perm)]
    reduce_scatter x1 -> x0, waiting for transfers between devices: 113 us -> none  [shards(): share = lax.psum_scatter(totals, 'spot', scatter_dimension=1, tiled=True)]
    all_gather x0 -> x3, blocking collectives: none -> 92.4 us  [the longest x1 74.6 us: mirrored_shards(): panels = lax.all_gather(jnp.stack([gap_here, scale]), 'gene', axis=0)]
    convert_element_type x3 -> x9, other arithmetic: 56.7 us -> 20.5 us  [the longest x4 14.1 us: mirrored_shards(): narrow = lambda a: a.astype(jnp.bfloat16)]
    select_n x1 -> x16, other arithmetic: 0.09 us -> 32.6 us  [the longest x1 8.55 us: mirrored_shards(): jnp.where(flag, jnp.concatenate([a, b], dim), jnp.concatenate([b, a], dim))]
    ppermute x4 -> x24, starting transfers between devices: 12.6 us -> 44.7 us  [the longest x11 22.1 us: mirrored_shards(): along = lambda a, perm: lax.ppermute(a, 'gene', perm)]
    psum x2 -> x0, blocking collectives: 25 us -> none  [the longest x1 12.7 us: shards(): lax.psum(jnp.sum(centred * centred, axis=(0, 1)), 'spot') / tissue_count]
  transfers between devices with their start and end apart: 6 -> 24, of which waited for: 4 -> 9; matrix products, arithmetic and copies ran while one was open for 2% -> 15% of each run, Pallas kernels for 0% -> 0%
where the time goes in v1:
time: 495 us; the launch traced here: 491 us
  waiting for transfers between devices  172 us (35%)
  blocking collectives  92.4 us (19%)
  other arithmetic  70.9 us (14%)
  matrix products  45.9 us (9%)
  starting transfers between devices  44.7 us (9%)
  local copies, waits for them, and re-layouts  40.9 us (8%)
  Pallas kernels  21.3 us (4%)
    all_gather x1, blocking collectives, mirrored_shards(): panels = lax.all_gather(jnp.stack([gap_here, scale]), 'gene', axis=0)  74.6 us
    ppermute x11, waiting for transfers between devices, mirrored_shards(): along = lambda a, perm: lax.ppermute(a, 'gene', perm)  54.5 us
    ppermute x1, waiting for transfers between devices, mirrored_shards(): lax.ppermute(jnp.where(first, bottom_n, top_n), ('spot', 'gene'), other_c...  50.8 us
    dot_general x6, matrix products, cross_panel(): lax.dot_general(left, right, contract_bins, preferred_element_type=jnp.fl...  45.9 us
    ppermute x1, waiting for transfers between devices, mirrored_shards(): below = lax.ppermute(dev[:2], 'spot', [(i + 2, i) for i in range(steps)])  23.4 us
    ppermute x11, starting transfers between devices, mirrored_shards(): along = lambda a, perm: lax.ppermute(a, 'gene', perm)  22.1 us
    pallas_call x1, Pallas kernels, lag_call(): pl.pallas_call(lag_kernel, out_shape=jax.ShapeDtypeStruct((rows, tall, ge...  21.3 us
    ppermute x1, waiting for transfers between devices, mirrored_shards(): above = lax.ppermute(dev[-2:], 'spot', [(i, i + 2) for i in range(steps)])  20.9 us
  transfers between devices with their start and end apart: 24, of which 9 were waited for; matrix products, arithmetic and copies ran while one was open for 15% of the time, Pallas kernels for 0%

profile of v1, /device:TPU:3, one launch (start us, length us, event | category | flops | bytes accessed | tf_op | source)
XLA Modules:
  0.0 490.5 jit_solution(6002648279028446344)
XLA Ops:
  0.0 3.9 multiply_convert_fusion.1
  7.3 9.5 %all-gather.2 = s32[8,4,512]{2,1,0:T(4,128)S(1)} all-gather(s32[1,4,512]{2,1,0:T(4,128)S(1)} %bitcast.121), channel_id=1, replica_groups=mesh['spot'=8,'gene'=4] {'spot'}, dimensions={0}, use_global_device_ids=true | all-gather | bytes 73728 | tf_op jit(solution)/shard_map/all_gather | solution.py:185
  20.6 4.3 convert_reduce_fusion.1
  24.9 4.5 convert_reduce_fusion
  29.5 8.2 %all-gather.3 = f32[8,4,512]{2,1,0:T(4,128)S(1)} all-gather(f32[1,4,512]{2,1,0:T(4,128)S(1)} %maximum_bitcast_fusion), channel_id=2, replica_groups=mesh['spot'=8,'gene'=4] {'spot'}, dimensions={0}, use_global_device_ids=true | all-gather | bytes 73728 | tf_op jit(solution)/shard_map/all_gather | solution.py:195
  37.9 3.1 collective-permute-start.2
  43.5 20.9 %collective-permute-done.2 = bf16[2,512,512]{2,1,0:T(8,128)(2,1)S(1)} collective-permute-done((bf16[2,512,512]{2,1,0:T(8,128)(2,1)S(1)}, bf16[2,512,512]{2,1,0:T(8,128)(2,1)S(1)}, u32[]{:S(2)}, u32[]{:S(2)}) %collective-permute-start.2) | collective-permute-done | bytes 1048608 | tf_op jit(solution)/shard_map/ppermute | solution.py:182
  64.4 23.4 %collective-permute-done.3 = bf16[2,512,512]{2,1,0:T(8,128)(2,1)S(1)} collective-permute-done((bf16[2,512,512]{2,1,0:T(8,128)(2,1)S(1)}, bf16[2,512,512]{2,1,0:T(8,128)(2,1)S(1)}, u32[]{:S(2)}, u32[]{:S(2)}) %collective-permute-start.3) | collective-permute-done | bytes 1048608 | tf_op jit(solution)/shard_map/ppermute | solution.py:183
  90.1 21.3 %shard_map.37 = bf16[8,784,512]{2,1,0:T(8,128)(2,1)} custom-call(f32[8,5]{1,0:T(8,128)S(1)} %stack.56.row_same, bf16[12,512,512]{2,1,0:T(8,128)(2,1)S(1)} %multiply_convert_fusion.z_ref, bf16[3,784,512]{2,1,0:T(8,128)(2,1)S(1)} %maximum_maximum_fusion.mat_ref), custom_call_target="tpu_custom_call" | custom-call | flops 16441671680 | bytes 12582912 | tf_op jit(solution)/shard_map/pallas_call | solution.py:111
  113.8 3.3 collective-permute-start.6
  121.8 19.2 %collective-permute-done.6 = bf16[4,272,512]{2,1,0:T(8,128)(2,1)S(1)} collective-permute-done((bf16[4,272,512]{2,1,0:T(8,128)(2,1)S(1)}, bf16[4,272,512]{2,1,0:T(8,128)(2,1)S(1)}, u32[]{:S(2)}, u32[]{:S(2)}) %collective-permute-start.6) | collective-permute-done | bytes 1114144 | tf_op jit(solution)/shard_map/ppermute | solution.py:149
  142.6 22.3 %collective-permute-done.5 = bf16[4,272,512]{2,1,0:T(8,128)(2,1)S(1)} collective-permute-done((bf16[4,272,512]{2,1,0:T(8,128)(2,1)}, bf16[4,272,512]{2,1,0:T(8,128)(2,1)S(1)}, u32[]{:S(2)}, u32[]{:S(2)}) %collective-permute-start.5) | collective-permute-done | bytes 1114144 | tf_op jit(solution)/shard_map/ppermute | solution.py:149
  169.4 3.7 slice_select_fusion.1
  174.3 74.6 %all-gather.4 = f32[4,2,512]{2,1,0:T(2,128)S(1)} all-gather(f32[1,2,512]{2,1,0:T(2,128)S(1)} %maximum_bitcast_fusion.1), channel_id=3, replica_groups=mesh['spot'=8,'gene'=4] {'gene'}, dimensions={0}, use_global_device_ids=true | all-gather | bytes 20480 | tf_op jit(solution)/shard_map/all_gather | solution.py:251
  250.5 5.6 %collective-permute-start.7 = (bf16[8,240,512]{2,1,0:T(8,128)(2,1)}, bf16[8,240,512]{2,1,0:T(8,128)(2,1)}, u32[]{:S(2)}, u32[]{:S(2)}) collective-permute-start(bf16[8,240,512]{2,1,0:T(8,128)(2,1)} %slice_select_fusion.1), channel_id=1, source_target_pairs={{0,1},{3,2},{4,5},{7,6},{8,9},{11,10},{12,13},{15,14},{16,17},{19,... | collective-permute-start | bytes 5898248 | tf_op jit(solution)/shard_map/ppermute | solution.py:149
  260.8 13.0 %collective-permute-done.13 = bf16[4,272,512]{2,1,0:T(8,128)(2,1)S(1)} collective-permute-done((bf16[4,272,512]{2,1,0:T(8,128)(2,1)}, bf16[4,272,512]{2,1,0:T(8,128)(2,1)S(1)}, u32[]{:S(2)}, u32[]{:S(2)}) %collective-permute-start.13) | collective-permute-done | bytes 1114144 | tf_op jit(solution)/shard_map/ppermute | solution.py:149
  274.9 8.6 %maximum_select_fusion = bf16[8,784,1024]{2,1,0:T(8,128)(2,1)S(1)} fusion(bf16[8,784,512]{2,1,0:T(8,128)(2,1)} %collective-permute-done.4, bf16[8,784,512]{2,1,0:T(8,128)(2,1)S(1)} %bitcast.119, pred[]{:T(512)S(6)} %eq.239), kind=kLoop, calls=%fused_computation | loop fusion | flops 57802752 | bytes 25690112 | tf_op jit(solution)/shard_map/jit(_where)/select_n | solution.py:150
  283.5 4.6 copy-done.2
  291.3 9.7 %fusion.30 = f32[1024,512]{1,0:T(8,128)S(1)} fusion(f32[1024,512]{1,0:T(8,128)} %copy.168, bf16[8,512,512]{2,1,0:T(8,128)(2,1)} %copy-done, bf16[8,784,1024]{2,1,0:T(8,128)(2,1)} %copy-done.2, f32[512]{0:T(512)S(1)} %bitcast.140), kind=kOutput, calls=%fused_computation.46 | convolution fusion | flops 4296015872 | bytes 16779264 | tf_op jit(solution)/shard_map/dot_general | solution.py:35
  303.0 3.1 fusion.16
  306.1 9.0 %fusion.29 = f32[1024,512]{0,1:T(8,128)S(1)} fusion(bf16[8,240,512]{2,1,0:T(8,128)(2,1)} %collective-permute-done.7, bf16[8,272,512]{2,1,0:T(8,128)(2,1)S(1)} %copy-done.15, pred[]{:T(512)S(6)} %lt.64, bf16[8,784,1024]{2,1,0:T(8,128)(2,1)} %copy-done.2, f32[512]{0:T(512)S(1)} %bitcast.139, f32[512]{0:T(512)S(1)} %bitcast.138, f32[1024]{0:T(1024)S(1)} %bitcast.133, ...), kind=kOutput, calls=%fused_computation.44 | convolution fusion | flops 4315938816 | bytes 14688258 | tf_op jit(solution)/shard_map/dot_general | solution.py:35
  317.2 15.4 %fusion.18 = f32[1024,512,1]{0,1,2:T(8,128)S(1)} fusion(bf16[8,784,1024]{2,1,0:T(8,128)(2,1)} %copy-done.2, bf16[4,272,512]{2,1,0:T(8,128)(2,1)} %broadcast_select_fusion.2, bf16[4,272,512]{2,1,0:T(8,128)(2,1)} %broadcast_select_fusion.3), kind=kOutput, calls=%fused_computation.27 | convolution fusion | flops 2282815488 | bytes 8781824 | tf_op jit(solution)/shard_map/dot_general | solution.py:35
  332.7 7.5 %broadcast_select_fusion.8 = (f32[1024,512]{0,1:T(8,128)}, f32[1024,512]{0,1:T(8,128)}, f32[1024,512]{0,1:T(8,128)S(1)}) fusion(pred[]{:T(512)S(6)} %lt.64, f32[1024,512]{0,1:T(8,128)S(1)} %copy-done.10, f32[1024,512]{0,1:T(8,128)} %copy-done.11, pred[]{:T(512)S(6)} %eq.238, f32[512]{0:T(512)S(1)} %bitcast.136, f32[512]{0:T(512)S(1)} %bitcast.134, ...), kind=kOutput, calls=%fused_computation.82 | convolution fusion | flops 2288582656 | bytes 19279874 | tf_op jit(solution)/shard_map/dot_general | solution.py:35
  342.1 5.0 %broadcast_select_fusion.4 = (f32[1024,512]{1,0:T(8,128)}, f32[1024,512]{1,0:T(8,128)}) fusion(f32[1024,512]{1,0:T(8,128)} %copy.178, pred[]{:T(512)S(6)} %lt.64, f32[1024,512]{1,0:T(8,128)} %copy.175, f32[1024,512]{1,0:T(8,128)} %copy-done.8, pred[]{:T(512)S(6)} %eq.238), kind=kLoop, calls=%fused_computation.78 | loop fusion | flops 1048576 | bytes 10485762 | tf_op jit(solution)/shard_map/jit(_where)/select_n | solution.py:272
  355.3 3.9 select_convert_fusion.5
  368.8 11.0 %collective-permute-done.17 = bf16[512,512]{0,1:T(8,128)(2,1)} collective-permute-done((bf16[512,512]{0,1:T(8,128)(2,1)}, bf16[512,512]{0,1:T(8,128)(2,1)}, u32[]{:S(2)}, u32[]{:S(2)}) %collective-permute-start.17) | collective-permute-done | bytes 524320 | tf_op jit(solution)/shard_map/ppermute | solution.py:148
  379.8 5.3 %select_convert_fusion.3 = (bf16[512,512]{0,1:T(8,128)(2,1)}, f32[512,512]{0,1:T(8,128)}, f32[512,512]{0,1:T(8,128)}) fusion(pred[]{:T(512)S(6)} %eq.236, bf16[512,512]{0,1:T(8,128)(2,1)} %collective-permute-done.17, f32[512,512]{0,1:T(8,128)S(1)} %copy.204, f32[1024,512]{0,1:T(8,128)S(1)} %broadcast_select_fusion.7, pred[]{:T(512)S(6)} %eq.237, ...), kind=kLoop, calls=%fused_computation.68 | loop fusion | flops 3145728 | bytes 12582914 | tf_op jit(solution)/shard_map/convert_element_type | solution.py:274
  405.7 3.7 broadcast_select_fusion.11
  410.4 9.2 %collective-permute-start.23 = (bf16[512,512]{0,1:T(8,128)(2,1)}, bf16[512,512]{0,1:T(8,128)(2,1)}, u32[]{:S(2)}, u32[]{:S(2)}) collective-permute-start(bf16[512,512]{0,1:T(8,128)(2,1)} %broadcast_select_fusion.10), channel_id=1, source_target_pairs={{1,12},{2,20},{3,28},{5,8},{6,16},{7,24},{8,5},{10,21},{11,29},{12... | collective-permute-start | bytes 1572872 | tf_op jit(solution)/shard_map/ppermute | solution.py:294
  419.6 3.1 collective-permute-start.22
  425.2 50.8 %collective-permute-done.23 = bf16[512,512]{0,1:T(8,128)(2,1)} collective-permute-done((bf16[512,512]{0,1:T(8,128)(2,1)}, bf16[512,512]{0,1:T(8,128)(2,1)}, u32[]{:S(2)}, u32[]{:S(2)}) %collective-permute-start.23) | collective-permute-done | bytes 524320 | tf_op jit(solution)/shard_map/ppermute | solution.py:294
  476.1 11.2 %collective-permute-done.22 = bf16[512,512]{0,1:T(8,128)(2,1)} collective-permute-done((bf16[512,512]{0,1:T(8,128)(2,1)}, bf16[512,512]{0,1:T(8,128)(2,1)}, u32[]{:S(2)}, u32[]{:S(2)}) %collective-permute-start.22) | collective-permute-done | bytes 524320 | tf_op jit(solution)/shard_map/ppermute | solution.py:293
  (152 shorter events, 86.5 us)
Async XLA Ops:
  6.5 14.1 %collective-permute-start = (bf16[4,512,512]{2,1,0:T(8,128)(2,1)}, bf16[4,512,512]{2,1,0:T(8,128)(2,1)}, u32[]{:S(2)}, u32[]{:S(2)}) collective-permute-start(bf16[4,512,512]{2,1,0:T(8,128)(2,1)} %get-tuple-element.25), channel_id=1, source_target_pairs={{0,4},{4,0},{8,12},{12,8},{16,20},{20,16},{24,28},{28,24},{1,5},{5... | collective-permute-start | bytes 6291464 | tf_op jit(solution)/shard_map/ppermute | solution.py:148
  7.2 11.5 %collective-permute-start.1 = (s32[4,512]{1,0:T(4,128)S(1)}, s32[4,512]{1,0:T(4,128)S(1)}, u32[]{:S(2)}, u32[]{:S(2)}) collective-permute-start(s32[4,512]{1,0:T(4,128)S(1)} %multiply_add_fusion), channel_id=1, source_target_pairs={{0,4},{4,0},{8,12},{12,8},{16,20},{20,16},{24,28},{28,24},{1,5},{5... | collective-permute-start | bytes 24584 | tf_op jit(solution)/shard_map/ppermute | solution.py:148
  29.4 83.0 %copy-start = (bf16[8,512,512]{2,1,0:T(8,128)(2,1)}, bf16[8,512,512]{2,1,0:T(8,128)(2,1)S(1)}, u32[]{:S(2)}) copy-start(bf16[8,512,512]{2,1,0:T(8,128)(2,1)S(1)} %get-tuple-element.17) | copy-start | bytes 12582916
  37.9 26.5 %collective-permute-start.2 = (bf16[2,512,512]{2,1,0:T(8,128)(2,1)S(1)}, bf16[2,512,512]{2,1,0:T(8,128)(2,1)S(1)}, u32[]{:S(2)}, u32[]{:S(2)}) collective-permute-start(bf16[2,512,512]{2,1,0:T(8,128)(2,1)S(1)} %get-tuple-element.23), channel_id=1, source_target_pairs={{0,8},{4,12},{8,16},{12,20},{16,24},{20,28},{1,9},{5,13},{9,17},{1... | collective-permute-start | bytes 3145736 | tf_op jit(solution)/shard_map/ppermute | solution.py:182
  41.0 46.8 %collective-permute-start.3 = (bf16[2,512,512]{2,1,0:T(8,128)(2,1)S(1)}, bf16[2,512,512]{2,1,0:T(8,128)(2,1)S(1)}, u32[]{:S(2)}, u32[]{:S(2)}) collective-permute-start(bf16[2,512,512]{2,1,0:T(8,128)(2,1)S(1)} %get-tuple-element.24), channel_id=1, source_target_pairs={{8,0},{12,4},{16,8},{20,12},{24,16},{28,20},{9,1},{13,5},{17,9},{2... | collective-permute-start | bytes 3145736 | tf_op jit(solution)/shard_map/ppermute | solution.py:183
  111.4 163.4 %collective-permute-start.4 = (bf16[8,784,512]{2,1,0:T(8,128)(2,1)}, bf16[8,784,512]{2,1,0:T(8,128)(2,1)}, u32[]{:S(2)}, u32[]{:S(2)}) collective-permute-start(bf16[8,784,512]{2,1,0:T(8,128)(2,1)} %shard_map.37), channel_id=1, source_target_pairs={{0,4},{4,0},{8,12},{12,8},{16,20},{20,16},{24,28},{28,24},{1,5},{5... | collective-permute-start | bytes 19267592 | tf_op jit(solution)/shard_map/ppermute | solution.py:148
  113.8 27.2 %collective-permute-start.6 = (bf16[4,272,512]{2,1,0:T(8,128)(2,1)S(1)}, bf16[4,272,512]{2,1,0:T(8,128)(2,1)S(1)}, u32[]{:S(2)}, u32[]{:S(2)}) collective-permute-start(bf16[4,272,512]{2,1,0:T(8,128)(2,1)S(1)} %get-tuple-element.28), channel_id=1, source_target_pairs={{0,1},{3,2},{4,5},{7,6},{8,9},{11,10},{12,13},{15,14},{16,17},{19,... | collective-permute-start | bytes 3342344 | tf_op jit(solution)/shard_map/ppermute | solution.py:149
  117.1 47.9 %collective-permute-start.5 = (bf16[4,272,512]{2,1,0:T(8,128)(2,1)}, bf16[4,272,512]{2,1,0:T(8,128)(2,1)S(1)}, u32[]{:S(2)}, u32[]{:S(2)}) collective-permute-start(bf16[4,272,512]{2,1,0:T(8,128)(2,1)} %get-tuple-element.27), channel_id=1, source_target_pairs={{0,1},{3,2},{4,5},{7,6},{8,9},{11,10},{12,13},{15,14},{16,17},{19,... | collective-permute-start | bytes 3342344 | tf_op jit(solution)/shard_map/ppermute | solution.py:149
  118.5 48.2 %collective-permute-start.10 = (bf16[4,272,512]{2,1,0:T(8,128)(2,1)S(1)}, bf16[4,272,512]{2,1,0:T(8,128)(2,1)}, u32[]{:S(2)}, u32[]{:S(2)}) collective-permute-start(bf16[4,272,512]{2,1,0:T(8,128)(2,1)S(1)} %get-tuple-element.28), channel_id=1, source_target_pairs={{1,2},{2,1},{5,6},{6,5},{9,10},{10,9},{13,14},{14,13},{17,18},{18,... | collective-permute-start | bytes 3342344 | tf_op jit(solution)/shard_map/ppermute | solution.py:149
  120.2 47.9 %collective-permute-start.8 = (bf16[4,272,512]{2,1,0:T(8,128)(2,1)}, bf16[4,272,512]{2,1,0:T(8,128)(2,1)}, u32[]{:S(2)}, u32[]{:S(2)}) collective-permute-start(bf16[4,272,512]{2,1,0:T(8,128)(2,1)} %get-tuple-element.27), channel_id=1, source_target_pairs={{1,2},{2,1},{5,6},{6,5},{9,10},{10,9},{13,14},{14,13},{17,18},{18,... | collective-permute-start | bytes 3342344 | tf_op jit(solution)/shard_map/ppermute | solution.py:149
  141.0 32.0 %collective-permute-start.14 = (bf16[4,272,512]{2,1,0:T(8,128)(2,1)S(1)}, bf16[4,272,512]{2,1,0:T(8,128)(2,1)}, u32[]{:S(2)}, u32[]{:S(2)}) collective-permute-start(bf16[4,272,512]{2,1,0:T(8,128)(2,1)S(1)} %collective-permute-done.6), channel_id=1, source_target_pairs={{1,2},{2,1},{5,6},{6,5},{9,10},{10,9},{13,14},{14,13},{17,18},{18,... | collective-permute-start | bytes 3342344 | tf_op jit(solution)/shard_map/ppermute | solution.py:149
  165.0 84.0 %collective-permute-start.12 = (bf16[4,272,512]{2,1,0:T(8,128)(2,1)S(1)}, bf16[4,272,512]{2,1,0:T(8,128)(2,1)}, u32[]{:S(2)}, u32[]{:S(2)}) collective-permute-start(bf16[4,272,512]{2,1,0:T(8,128)(2,1)S(1)} %collective-permute-done.5), channel_id=1, source_target_pairs={{1,2},{2,1},{5,6},{6,5},{9,10},{10,9},{13,14},{14,13},{17,18},{18,... | collective-permute-start | bytes 3342344 | tf_op jit(solution)/shard_map/ppermute | solution.py:149
  166.7 83.8 %collective-permute-start.11 = (bf16[4,272,512]{2,1,0:T(8,128)(2,1)}, bf16[4,272,512]{2,1,0:T(8,128)(2,1)}, u32[]{:S(2)}, u32[]{:S(2)}) collective-permute-start(bf16[4,272,512]{2,1,0:T(8,128)(2,1)} %collective-permute-done.10), channel_id=1, source_target_pairs={{1,0},{2,3},{5,4},{6,7},{9,8},{10,11},{13,12},{14,15},{17,16},{18,... | collective-permute-start | bytes 3342344 | tf_op jit(solution)/shard_map/ppermute | solution.py:149
  168.1 90.4 %collective-permute-start.9 = (bf16[4,272,512]{2,1,0:T(8,128)(2,1)}, bf16[4,272,512]{2,1,0:T(8,128)(2,1)S(1)}, u32[]{:S(2)}, u32[]{:S(2)}) collective-permute-start(bf16[4,272,512]{2,1,0:T(8,128)(2,1)} %collective-permute-done.8), channel_id=1, source_target_pairs={{1,0},{2,3},{5,4},{6,7},{9,8},{10,11},{13,12},{14,15},{17,16},{18,... | collective-permute-start | bytes 3342344 | tf_op jit(solution)/shard_map/ppermute | solution.py:149
  173.0 86.6 %collective-permute-start.15 = (bf16[4,272,512]{2,1,0:T(8,128)(2,1)}, bf16[4,272,512]{2,1,0:T(8,128)(2,1)S(1)}, u32[]{:S(2)}, u32[]{:S(2)}) collective-permute-start(bf16[4,272,512]{2,1,0:T(8,128)(2,1)} %collective-permute-done.14), channel_id=1, source_target_pairs={{1,0},{2,3},{5,4},{6,7},{9,8},{10,11},{13,12},{14,15},{17,16},{18,... | collective-permute-start | bytes 3342344 | tf_op jit(solution)/shard_map/ppermute | solution.py:149
  249.0 24.8 %collective-permute-start.13 = (bf16[4,272,512]{2,1,0:T(8,128)(2,1)}, bf16[4,272,512]{2,1,0:T(8,128)(2,1)S(1)}, u32[]{:S(2)}, u32[]{:S(2)}) collective-permute-start(bf16[4,272,512]{2,1,0:T(8,128)(2,1)} %collective-permute-done.12), channel_id=1, source_target_pairs={{1,0},{2,3},{5,4},{6,7},{9,8},{10,11},{13,12},{14,15},{17,16},{18,... | collective-permute-start | bytes 3342344 | tf_op jit(solution)/shard_map/ppermute | solution.py:149
  250.4 24.5 %slice-start = ((s8[6422528]{0:T(1024)(128)(4,1)}), s8[4194304]{0:T(1024)(128)(4,1)S(1)}, s32[]{:S(2)}) async-start(s8[6422528]{0:T(1024)(128)(4,1)} %bitcast.118), calls=%async_computation | async-start | bytes 8388608
  250.5 55.6 %collective-permute-start.7 = (bf16[8,240,512]{2,1,0:T(8,128)(2,1)}, bf16[8,240,512]{2,1,0:T(8,128)(2,1)}, u32[]{:S(2)}, u32[]{:S(2)}) collective-permute-start(bf16[8,240,512]{2,1,0:T(8,128)(2,1)} %slice_select_fusion.1), channel_id=1, source_target_pairs={{0,1},{3,2},{4,5},{7,6},{8,9},{11,10},{12,13},{15,14},{16,17},{19,... | collective-permute-start | bytes 5898248 | tf_op jit(solution)/shard_map/ppermute | solution.py:149
  258.5 16.4 %slice-start.1 = ((s8[6422528]{0:T(1024)(128)(4,1)}), s8[2228224]{0:T(1024)(128)(4,1)S(1)}, s32[]{:S(2)}) async-start(s8[6422528]{0:T(1024)(128)(4,1)} %bitcast.118), calls=%async_computation.1 | async-start | bytes 4456448
  315.2 17.4 %copy-start.11 = (f32[1024,512]{0,1:T(8,128)}, f32[1024,512]{0,1:T(8,128)S(1)}, u32[]{:S(2)}) copy-start(f32[1024,512]{0,1:T(8,128)S(1)} %fusion.29) | copy-start | bytes 6291460
  317.2 15.4 %copy-start.10 = (f32[1024,512]{0,1:T(8,128)S(1)}, f32[1024,512]{0,1:T(8,128)}, u32[]{:S(2)}) copy-start(f32[1024,512]{0,1:T(8,128)} %copy.171) | copy-start | bytes 6291460
  317.2 15.4 %copy-start.12 = (bf16[4,272,512]{2,1,0:T(8,128)(2,1)S(1)}, bf16[4,272,512]{2,1,0:T(8,128)(2,1)}, u32[]{:S(2)}) copy-start(bf16[4,272,512]{2,1,0:T(8,128)(2,1)} %broadcast_select_fusion) | copy-start | bytes 3342340
  317.2 15.4 %copy-start.13 = (bf16[4,272,512]{2,1,0:T(8,128)(2,1)S(1)}, bf16[4,272,512]{2,1,0:T(8,128)(2,1)}, u32[]{:S(2)}) copy-start(bf16[4,272,512]{2,1,0:T(8,128)(2,1)} %broadcast_select_fusion.1) | copy-start | bytes 3342340
  359.2 9.6 %collective-permute-start.16 = (bf16[512,512]{0,1:T(8,128)(2,1)}, bf16[512,512]{0,1:T(8,128)(2,1)}, u32[]{:S(2)}, u32[]{:S(2)}) collective-permute-start(bf16[512,512]{0,1:T(8,128)(2,1)} %get-tuple-element.30), channel_id=1, source_target_pairs={{0,16},{4,20},{8,24},{12,28},{16,0},{20,4},{24,8},{28,12},{1,17},{... | collective-permute-start | bytes 1572872 | tf_op jit(solution)/shard_map/ppermute | solution.py:148
  359.2 20.7 %collective-permute-start.17 = (bf16[512,512]{0,1:T(8,128)(2,1)}, bf16[512,512]{0,1:T(8,128)(2,1)}, u32[]{:S(2)}, u32[]{:S(2)}) collective-permute-start(bf16[512,512]{0,1:T(8,128)(2,1)} %get-tuple-element.32), channel_id=1, source_target_pairs={{0,16},{4,20},{8,24},{12,28},{16,0},{20,4},{24,8},{28,12},{1,17},{... | collective-permute-start | bytes 1572872 | tf_op jit(solution)/shard_map/ppermute | solution.py:148
  360.6 19.2 %collective-permute-start.19 = (bf16[512,512]{0,1:T(8,128)(2,1)}, bf16[512,512]{0,1:T(8,128)(2,1)}, u32[]{:S(2)}, u32[]{:S(2)}) collective-permute-start(bf16[512,512]{0,1:T(8,128)(2,1)} %get-tuple-element.31), channel_id=1, source_target_pairs={{0,8},{4,12},{8,0},{12,4},{16,24},{20,28},{24,16},{28,20},{1,9},{5... | collective-permute-start | bytes 1572872 | tf_op jit(solution)/shard_map/ppermute | solution.py:148
  365.2 24.7 %collective-permute-start.20 = (bf16[512,512]{1,0:T(8,128)(2,1)}, bf16[512,512]{1,0:T(8,128)(2,1)}, u32[]{:S(2)}, u32[]{:S(2)}) collective-permute-start(bf16[512,512]{1,0:T(8,128)(2,1)} %select_convert_fusion.1), channel_id=1, source_target_pairs={{0,8},{4,12},{8,0},{12,4},{16,24},{20,28},{24,16},{28,20},{1,9},{5... | collective-permute-start | bytes 1572872 | tf_op jit(solution)/shard_map/ppermute | solution.py:148
  392.6 8.3 %collective-permute-start.21 = (bf16[512,512]{1,0:T(8,128)(2,1)}, bf16[512,512]{1,0:T(8,128)(2,1)}, u32[]{:S(2)}, u32[]{:S(2)}) collective-permute-start(bf16[512,512]{1,0:T(8,128)(2,1)} %get-tuple-element.9), channel_id=1, source_target_pairs={{0,16},{4,20},{8,24},{12,28},{16,0},{20,4},{24,8},{28,12},{1,17},{... | collective-permute-start | bytes 1572872 | tf_op jit(solution)/shard_map/ppermute | solution.py:148
  395.6 10.1 %collective-permute-start.18 = (bf16[512,512]{0,1:T(8,128)(2,1)}, bf16[512,512]{0,1:T(8,128)(2,1)}, u32[]{:S(2)}, u32[]{:S(2)}) collective-permute-start(bf16[512,512]{0,1:T(8,128)(2,1)} %get-tuple-element.21), channel_id=1, source_target_pairs={{0,8},{4,12},{8,0},{12,4},{16,24},{20,28},{24,16},{28,20},{1,9},{5... | collective-permute-start | bytes 1572872 | tf_op jit(solution)/shard_map/ppermute | solution.py:148
  410.4 65.7 %collective-permute-start.23 = (bf16[512,512]{0,1:T(8,128)(2,1)}, bf16[512,512]{0,1:T(8,128)(2,1)}, u32[]{:S(2)}, u32[]{:S(2)}) collective-permute-start(bf16[512,512]{0,1:T(8,128)(2,1)} %broadcast_select_fusion.10), channel_id=1, source_target_pairs={{1,12},{2,20},{3,28},{5,8},{6,16},{7,24},{8,5},{10,21},{11,29},{12... | collective-permute-start | bytes 1572872 | tf_op jit(solution)/shard_map/ppermute | solution.py:294
  419.6 67.7 %collective-permute-start.22 = (bf16[512,512]{0,1:T(8,128)(2,1)}, bf16[512,512]{0,1:T(8,128)(2,1)}, u32[]{:S(2)}, u32[]{:S(2)}) collective-permute-start(bf16[512,512]{0,1:T(8,128)(2,1)} %get-tuple-element.7), channel_id=1, source_target_pairs={{1,8},{2,16},{3,24},{5,12},{6,20},{7,28},{8,1},{10,17},{11,25},{12... | collective-permute-start | bytes 1572872 | tf_op jit(solution)/shard_map/ppermute | solution.py:293
  422.8 64.5 %copy-start.6 = (f32[512,512]{1,0:T(8,128)S(1)}, f32[512,512]{1,0:T(8,128)}, u32[]{:S(2)}) copy-start(f32[512,512]{1,0:T(8,128)} %convert_add_fusion) | copy-start | bytes 3145732
  (12 other events, 55.4 us)

commit v2 on v1

--- a/solution.py
+++ b/solution.py
@@ -170,13 +170,6 @@
     mid, edge = cols // 2, 16
     part_a = jnp.where(low, dev[:, : mid + edge], dev[:, mid - edge :])
     part_b = jnp.where(low, dev[:, mid + edge :], dev[:, : mid - edge])
-    pieces = [part_a[:rows], part_a[rows:]]
-    in_a = [along(p, P_IN) for p in pieces]
-    cross_a = [along(p, P_CROSS) for p in pieces]
-    out_inner = [along(p, P_OUT) for p in cross_a]
-    cross_outer = [along(p, P_CROSS) for p in in_a]
-    in_b = along(part_b, P_IN)
-    out_outer = [along(p, P_OUT) for p in cross_outer]
 
     steps = spots - 2
     above = lax.ppermute(dev[-2:], "spot", [(i, i + 2) for i in range(steps)])
@@ -200,6 +193,16 @@
     gap = mean - shifts
     variance = jnp.sum(sum2 - 2.0 * gap * sum1 + bins * gap * gap, axis=0) / tissue_count
     scale = 1.0 / jnp.sqrt(variance + 1e-05)
+    panels = lax.all_gather(jnp.stack([lax.dynamic_index_in_dim(gap, chip, 0, keepdims=False), scale]), "gene", axis=0)
+    part_a, part_b, panels = lax.optimization_barrier((part_a, part_b, panels))
+    pieces = [part_a[:rows], part_a[rows:]]
+    in_a = [along(p, P_IN) for p in pieces]
+    cross_a = [along(p, P_CROSS) for p in pieces]
+    above, below, in_a, cross_a = lax.optimization_barrier((above, below, in_a, cross_a))
+    out_inner = [along(p, P_OUT) for p in cross_a]
+    cross_outer = [along(p, P_CROSS) for p in in_a]
+    in_b = along(part_b, P_IN)
+    out_outer = [along(p, P_OUT) for p in cross_outer]
     pair_norm = pair_sum(code_all, rows * spots, cols)
 
     band = 2 * rows
@@ -248,7 +251,6 @@
     lag_sum = lambda a, t: cross_panel(a, t.reshape(-1, 1).astype(jnp.bfloat16))
     sum_all, sum_part = lag_sum(lag_all, tissue_both), lag_sum(lag_part, tissue_part)
 
-    panels = lax.all_gather(jnp.stack([gap_here, scale]), "gene", axis=0)
     of_panel = lambda h: lax.dynamic_index_in_dim(panels, h, 0, keepdims=False)
 
     def settle(product, total, h):

time: 495 us -> 461 us (0.931)
  blocking collectives: 92.4 us -> 28.2 us
  starting transfers between devices: 44.7 us -> 66.6 us
  waiting for transfers between devices: 172 us -> 179 us
    all_gather x1, blocking collectives: 74.6 us -> 10.5 us  [mirrored_shards(): lax.all_gather(jnp.stack([lax.dynamic_index_in_dim(gap, chip, 0, keepdims...]
    ppermute x11, starting transfers between devices: 22.1 us -> 43.9 us  [mirrored_shards(): along = lambda a, perm: lax.ppermute(a, 'gene', perm)]
    ppermute x11, waiting for transfers between devices: 54.5 us -> 75.2 us  [mirrored_shards(): along = lambda a, perm: lax.ppermute(a, 'gene', perm)]
    ppermute x1, waiting for transfers between devices: 20.9 us -> 1.17 us  [mirrored_shards(): above = lax.ppermute(dev[-2:], 'spot', [(i, i + 2) for i in range(steps)])]
    ppermute x9, waiting for transfers between devices: 11.5 us -> 17.2 us  [mirrored_shards(): lax.ppermute(a, 'spot', [(i, i ^ bit) for i in range(spots)])]
  transfers between devices with their start and end apart: 24 -> 24, of which waited for: 9 -> 11; matrix products, arithmetic and copies ran while one was open for 15% -> 16% of each run, Pallas kernels for 0% -> 0%
where the time goes in v2:
time: 461 us; the launch traced here: 457 us
  waiting for transfers between devices  179 us (39%)
  other arithmetic  70.1 us (15%)
  starting transfers between devices  66.6 us (14%)
  matrix products  45.9 us (10%)
  local copies, waits for them, and re-layouts  43.9 us (10%)
  blocking collectives  28.2 us (6%)
  Pallas kernels  21.3 us (5%)
    ppermute x11, waiting for transfers between devices, mirrored_shards(): along = lambda a, perm: lax.ppermute(a, 'gene', perm)  75.2 us
    ppermute x1, waiting for transfers between devices, mirrored_shards(): lax.ppermute(jnp.where(first, bottom_n, top_n), ('spot', 'gene'), other_c...  51.7 us
    dot_general x6, matrix products, cross_panel(): lax.dot_general(left, right, contract_bins, preferred_element_type=jnp.fl...  45.9 us
    ppermute x11, starting transfers between devices, mirrored_shards(): along = lambda a, perm: lax.ppermute(a, 'gene', perm)  43.9 us
    ppermute x1, waiting for transfers between devices, mirrored_shards(): below = lax.ppermute(dev[:2], 'spot', [(i + 2, i) for i in range(steps)])  22.1 us
    pallas_call x1, Pallas kernels, lag_call(): pl.pallas_call(lag_kernel, out_shape=jax.ShapeDtypeStruct((rows, tall, ge...  21.3 us
    ppermute x9, waiting for transfers between devices, mirrored_shards(): lax.ppermute(a, 'spot', [(i, i ^ bit) for i in range(spots)])  17.2 us
    convert_element_type x4, other arithmetic, mirrored_shards(): narrow = lambda a: a.astype(jnp.bfloat16)  14.1 us
  transfers between devices with their start and end apart: 24, of which 11 were waited for; matrix products, arithmetic and copies ran while one was open for 16% of the time, Pallas kernels for 0%

profile of v2, /device:TPU:3, one launch (start us, length us, event | category | flops | bytes accessed | tf_op | source)
XLA Modules:
  0.0 456.7 jit_solution(3580008500363175975)
XLA Ops:
  0.0 3.9 multiply_convert_fusion.1
  6.6 9.5 %all-gather.2 = s32[8,4,512]{2,1,0:T(4,128)S(1)} all-gather(s32[1,4,512]{2,1,0:T(4,128)S(1)} %bitcast.121), channel_id=1, replica_groups=mesh['spot'=8,'gene'=4] {'spot'}, dimensions={0}, use_global_device_ids=true | all-gather | bytes 73728 | tf_op jit(solution)/shard_map/all_gather | solution.py:178
  21.4 4.5 convert_reduce_fusion
  26.0 8.2 %all-gather.3 = f32[8,4,512]{2,1,0:T(4,128)S(1)} all-gather(f32[1,4,512]{2,1,0:T(4,128)S(1)} %maximum_bitcast_fusion), channel_id=2, replica_groups=mesh['spot'=8,'gene'=4] {'spot'}, dimensions={0}, use_global_device_ids=true | all-gather | bytes 73728 | tf_op jit(solution)/shard_map/all_gather | solution.py:188
  35.5 3.1 collective-permute-start.2
  38.6 10.5 %all-gather.4 = f32[4,2,512]{2,1,0:T(2,128)S(1)} all-gather(f32[1,2,512]{2,1,0:T(2,128)S(1)} %maximum_bitcast_fusion.1), channel_id=3, replica_groups=mesh['spot'=8,'gene'=4] {'gene'}, dimensions={0}, use_global_device_ids=true | all-gather | bytes 20480 | tf_op jit(solution)/shard_map/all_gather | solution.py:196
  52.4 3.5 collective-permute-start.4
  66.4 22.1 %collective-permute-done.3 = bf16[2,512,512]{2,1,0:T(8,128)(2,1)} collective-permute-done((bf16[2,512,512]{2,1,0:T(8,128)(2,1)}, bf16[2,512,512]{2,1,0:T(8,128)(2,1)}, u32[]{:S(2)}, u32[]{:S(2)}) %collective-permute-start.3) | collective-permute-done | bytes 1048608 | tf_op jit(solution)/shard_map/ppermute | solution.py:176
  88.4 12.3 %collective-permute-done.5 = bf16[4,272,512]{2,1,0:T(8,128)(2,1)S(1)} collective-permute-done((bf16[4,272,512]{2,1,0:T(8,128)(2,1)}, bf16[4,272,512]{2,1,0:T(8,128)(2,1)S(1)}, u32[]{:S(2)}, u32[]{:S(2)}) %collective-permute-start.5) | collective-permute-done | bytes 1114144 | tf_op jit(solution)/shard_map/ppermute | solution.py:149
  100.7 3.7 multiply_convert_fusion.z_ref
  104.4 21.3 %shard_map.37 = bf16[8,784,512]{2,1,0:T(8,128)(2,1)} custom-call(f32[8,5]{1,0:T(8,128)S(1)} %stack.57.row_same, bf16[12,512,512]{2,1,0:T(8,128)(2,1)S(1)} %multiply_convert_fusion.z_ref, bf16[3,784,512]{2,1,0:T(8,128)(2,1)S(1)} %maximum_maximum_fusion.mat_ref), custom_call_target="tpu_custom_call" | custom-call | flops 16441671680 | bytes 12582912 | tf_op jit(solution)/shard_map/pallas_call | solution.py:111
  125.7 4.1 collective-permute-start.8
  140.1 24.5 %collective-permute-done.11 = bf16[4,272,512]{2,1,0:T(8,128)(2,1)} collective-permute-done((bf16[4,272,512]{2,1,0:T(8,128)(2,1)}, bf16[4,272,512]{2,1,0:T(8,128)(2,1)}, u32[]{:S(2)}, u32[]{:S(2)}) %collective-permute-start.11) | collective-permute-done | bytes 1114144 | tf_op jit(solution)/shard_map/ppermute | solution.py:149
  164.6 27.0 %collective-permute-start.9 = (bf16[8,240,512]{2,1,0:T(8,128)(2,1)}, bf16[8,240,512]{2,1,0:T(8,128)(2,1)}, u32[]{:S(2)}, u32[]{:S(2)}) collective-permute-start(bf16[8,240,512]{2,1,0:T(8,128)(2,1)} %slice_select_fusion.1), channel_id=1, source_target_pairs={{0,1},{3,2},{4,5},{7,6},{8,9},{11,10},{12,13},{15,14},{16,17},{19,... | collective-permute-start | bytes 5898248 | tf_op jit(solution)/shard_map/ppermute | solution.py:149
  196.5 15.7 %collective-permute-done.15 = bf16[4,272,512]{2,1,0:T(8,128)(2,1)S(1)} collective-permute-done((bf16[4,272,512]{2,1,0:T(8,128)(2,1)}, bf16[4,272,512]{2,1,0:T(8,128)(2,1)S(1)}, u32[]{:S(2)}, u32[]{:S(2)}) %collective-permute-start.15) | collective-permute-done | bytes 1114144 | tf_op jit(solution)/shard_map/ppermute | solution.py:149
  213.4 22.7 %collective-permute-done.13 = bf16[4,272,512]{2,1,0:T(8,128)(2,1)S(1)} collective-permute-done((bf16[4,272,512]{2,1,0:T(8,128)(2,1)}, bf16[4,272,512]{2,1,0:T(8,128)(2,1)S(1)}, u32[]{:S(2)}, u32[]{:S(2)}) %collective-permute-start.13) | collective-permute-done | bytes 1114144 | tf_op jit(solution)/shard_map/ppermute | solution.py:149
  237.2 8.4 %maximum_select_fusion = bf16[8,784,1024]{2,1,0:T(8,128)(2,1)S(1)} fusion(bf16[8,784,512]{2,1,0:T(8,128)(2,1)} %collective-permute-done.8, bf16[8,784,512]{2,1,0:T(8,128)(2,1)S(1)} %bitcast.119, pred[]{:T(512)S(6)} %eq.239), kind=kLoop, calls=%fused_computation | loop fusion | flops 57802752 | bytes 25690112 | tf_op jit(solution)/shard_map/jit(_where)/select_n | solution.py:150
  245.7 4.6 %copy-done.2 = bf16[8,784,1024]{2,1,0:T(8,128)(2,1)} copy-done((bf16[8,784,1024]{2,1,0:T(8,128)(2,1)}, bf16[8,784,1024]{2,1,0:T(8,128)(2,1)S(1)}, u32[]{:S(2)}) %copy-start.2) | copy-done | bytes 12845080
  253.5 9.7 %fusion.30 = f32[1024,512]{1,0:T(8,128)S(1)} fusion(f32[1024,512]{1,0:T(8,128)} %copy.168, bf16[8,512,512]{2,1,0:T(8,128)(2,1)} %copy-done, bf16[8,784,1024]{2,1,0:T(8,128)(2,1)} %copy-done.2, f32[512]{0:T(512)S(1)} %bitcast.140), kind=kOutput, calls=%fused_computation.46 | convolution fusion | flops 4296015872 | bytes 16779264 | tf_op jit(solution)/shard_map/dot_general | solution.py:35
  265.2 3.1 fusion.16
  268.4 9.1 %fusion.29 = f32[1024,512]{0,1:T(8,128)S(1)} fusion(bf16[8,240,512]{2,1,0:T(8,128)(2,1)} %collective-permute-done.9, bf16[8,272,512]{2,1,0:T(8,128)(2,1)S(1)} %copy-done.17, pred[]{:T(512)S(6)} %lt.66, bf16[8,784,1024]{2,1,0:T(8,128)(2,1)} %copy-done.2, f32[512]{0:T(512)S(1)} %bitcast.139, f32[512]{0:T(512)S(1)} %bitcast.138, f32[1024]{0:T(1024)S(1)} %bitcast.133, ...), kind=kOutput, calls=%fused_computation.44 | convolution fusion | flops 4315938816 | bytes 14688258 | tf_op jit(solution)/shard_map/dot_general | solution.py:35
  279.4 15.4 %fusion.18 = f32[1024,512,1]{0,1,2:T(8,128)S(1)} fusion(bf16[8,784,1024]{2,1,0:T(8,128)(2,1)} %copy-done.2, bf16[4,272,512]{2,1,0:T(8,128)(2,1)} %broadcast_select_fusion.2, bf16[4,272,512]{2,1,0:T(8,128)(2,1)} %broadcast_select_fusion.3), kind=kOutput, calls=%fused_computation.27 | convolution fusion | flops 2282815488 | bytes 8781824 | tf_op jit(solution)/shard_map/dot_general | solution.py:35
  294.9 7.5 %broadcast_select_fusion.8 = (f32[1024,512]{0,1:T(8,128)}, f32[1024,512]{0,1:T(8,128)}, f32[1024,512]{0,1:T(8,128)S(1)}) fusion(pred[]{:T(512)S(6)} %lt.66, f32[1024,512]{0,1:T(8,128)S(1)} %copy-done.10, f32[1024,512]{0,1:T(8,128)} %copy-done.11, pred[]{:T(512)S(6)} %eq.238, f32[512]{0:T(512)S(1)} %bitcast.136, f32[512]{0:T(512)S(1)} %bitcast.134, ...), kind=kOutput, calls=%fused_computation.82 | convolution fusion | flops 2288582656 | bytes 19279874 | tf_op jit(solution)/shard_map/dot_general | solution.py:35
  304.3 5.0 %broadcast_select_fusion.4 = (f32[1024,512]{1,0:T(8,128)}, f32[1024,512]{1,0:T(8,128)}) fusion(f32[1024,512]{1,0:T(8,128)} %copy.178, pred[]{:T(512)S(6)} %lt.66, f32[1024,512]{1,0:T(8,128)} %copy.175, f32[1024,512]{1,0:T(8,128)} %copy-done.8, pred[]{:T(512)S(6)} %eq.238), kind=kLoop, calls=%fused_computation.78 | loop fusion | flops 1048576 | bytes 10485762 | tf_op jit(solution)/shard_map/jit(_where)/select_n | solution.py:274
  317.5 3.8 select_convert_fusion.5
  333.9 11.2 %collective-permute-done.17 = bf16[512,512]{0,1:T(8,128)(2,1)} collective-permute-done((bf16[512,512]{0,1:T(8,128)(2,1)}, bf16[512,512]{0,1:T(8,128)(2,1)}, u32[]{:S(2)}, u32[]{:S(2)}) %collective-permute-start.17) | collective-permute-done | bytes 524320 | tf_op jit(solution)/shard_map/ppermute | solution.py:148
  345.2 5.3 %select_convert_fusion.3 = (bf16[512,512]{0,1:T(8,128)(2,1)}, f32[512,512]{0,1:T(8,128)}, f32[512,512]{0,1:T(8,128)}) fusion(pred[]{:T(512)S(6)} %eq.236, bf16[512,512]{0,1:T(8,128)(2,1)} %collective-permute-done.17, f32[512,512]{0,1:T(8,128)S(1)} %copy.204, f32[1024,512]{0,1:T(8,128)S(1)} %broadcast_select_fusion.7, pred[]{:T(512)S(6)} %eq.237, ...), kind=kLoop, calls=%fused_computation.68 | loop fusion | flops 3145728 | bytes 12582914 | tf_op jit(solution)/shard_map/convert_element_type | solution.py:276
  374.4 3.7 broadcast_select_fusion.11
  379.1 5.4 %collective-permute-start.23 = (bf16[512,512]{0,1:T(8,128)(2,1)}, bf16[512,512]{0,1:T(8,128)(2,1)}, u32[]{:S(2)}, u32[]{:S(2)}) collective-permute-start(bf16[512,512]{0,1:T(8,128)(2,1)} %broadcast_select_fusion.10), channel_id=1, source_target_pairs={{1,12},{2,20},{3,28},{5,8},{6,16},{7,24},{8,5},{10,21},{11,29},{12... | collective-permute-start | bytes 1572872 | tf_op jit(solution)/shard_map/ppermute | solution.py:296
  384.5 3.4 collective-permute-start.22
  390.5 51.7 %collective-permute-done.23 = bf16[512,512]{0,1:T(8,128)(2,1)} collective-permute-done((bf16[512,512]{0,1:T(8,128)(2,1)}, bf16[512,512]{0,1:T(8,128)(2,1)}, u32[]{:S(2)}, u32[]{:S(2)}) %collective-permute-start.23) | collective-permute-done | bytes 524320 | tf_op jit(solution)/shard_map/ppermute | solution.py:296
  442.2 11.2 %collective-permute-done.22 = bf16[512,512]{0,1:T(8,128)(2,1)} collective-permute-done((bf16[512,512]{0,1:T(8,128)(2,1)}, bf16[512,512]{0,1:T(8,128)(2,1)}, u32[]{:S(2)}, u32[]{:S(2)}) %collective-permute-start.22) | collective-permute-done | bytes 524320 | tf_op jit(solution)/shard_map/ppermute | solution.py:295
  (156 shorter events, 99.4 us)
Async XLA Ops:
  5.8 12.7 %collective-permute-start = (bf16[4,512,512]{2,1,0:T(8,128)(2,1)}, bf16[4,512,512]{2,1,0:T(8,128)(2,1)}, u32[]{:S(2)}, u32[]{:S(2)}) collective-permute-start(bf16[4,512,512]{2,1,0:T(8,128)(2,1)} %get-tuple-element.43), channel_id=1, source_target_pairs={{0,4},{4,0},{8,12},{12,8},{16,20},{20,16},{24,28},{28,24},{1,5},{5... | collective-permute-start | bytes 6291464 | tf_op jit(solution)/shard_map/ppermute | solution.py:148
  6.5 10.0 %collective-permute-start.1 = (s32[4,512]{1,0:T(4,128)S(1)}, s32[4,512]{1,0:T(4,128)S(1)}, u32[]{:S(2)}, u32[]{:S(2)}) collective-permute-start(s32[4,512]{1,0:T(4,128)S(1)} %multiply_add_fusion), channel_id=1, source_target_pairs={{0,4},{4,0},{8,12},{12,8},{16,20},{20,16},{24,28},{28,24},{1,5},{5... | collective-permute-start | bytes 24584 | tf_op jit(solution)/shard_map/ppermute | solution.py:148
  25.9 24.7 %copy-start = (bf16[8,512,512]{2,1,0:T(8,128)(2,1)}, bf16[8,512,512]{2,1,0:T(8,128)(2,1)S(1)}, u32[]{:S(2)}) copy-start(bf16[8,512,512]{2,1,0:T(8,128)(2,1)S(1)} %get-tuple-element.35) | copy-start | bytes 12582916
  35.5 26.5 %collective-permute-start.2 = (bf16[2,512,512]{2,1,0:T(8,128)(2,1)S(1)}, bf16[2,512,512]{2,1,0:T(8,128)(2,1)S(1)}, u32[]{:S(2)}, u32[]{:S(2)}) collective-permute-start(bf16[2,512,512]{2,1,0:T(8,128)(2,1)S(1)} %get-tuple-element.42), channel_id=1, source_target_pairs={{0,8},{4,12},{8,16},{12,20},{16,24},{20,28},{1,9},{5,13},{9,17},{1... | collective-permute-start | bytes 3145736 | tf_op jit(solution)/shard_map/ppermute | solution.py:175
  52.4 36.0 %collective-permute-start.4 = (bf16[4,272,512]{2,1,0:T(8,128)(2,1)}, bf16[4,272,512]{2,1,0:T(8,128)(2,1)S(1)}, u32[]{:S(2)}, u32[]{:S(2)}) collective-permute-start(bf16[4,272,512]{2,1,0:T(8,128)(2,1)} %get-tuple-element.46), channel_id=1, source_target_pairs={{0,1},{3,2},{4,5},{7,6},{8,9},{11,10},{12,13},{15,14},{16,17},{19,... | collective-permute-start | bytes 3342344 | tf_op jit(solution)/shard_map/ppermute | solution.py:149
  55.9 44.8 %collective-permute-start.6 = (bf16[4,272,512]{2,1,0:T(8,128)(2,1)}, bf16[4,272,512]{2,1,0:T(8,128)(2,1)}, u32[]{:S(2)}, u32[]{:S(2)}) collective-permute-start(bf16[4,272,512]{2,1,0:T(8,128)(2,1)} %get-tuple-element.46), channel_id=1, source_target_pairs={{1,2},{2,1},{5,6},{6,5},{9,10},{10,9},{13,14},{14,13},{17,18},{18,... | collective-permute-start | bytes 3342344 | tf_op jit(solution)/shard_map/ppermute | solution.py:149
  57.6 43.1 %collective-permute-start.5 = (bf16[4,272,512]{2,1,0:T(8,128)(2,1)}, bf16[4,272,512]{2,1,0:T(8,128)(2,1)S(1)}, u32[]{:S(2)}, u32[]{:S(2)}) collective-permute-start(bf16[4,272,512]{2,1,0:T(8,128)(2,1)} %get-tuple-element.45), channel_id=1, source_target_pairs={{0,1},{3,2},{4,5},{7,6},{8,9},{11,10},{12,13},{15,14},{16,17},{19,... | collective-permute-start | bytes 3342344 | tf_op jit(solution)/shard_map/ppermute | solution.py:149
  59.1 41.6 %collective-permute-start.7 = (bf16[4,272,512]{2,1,0:T(8,128)(2,1)}, bf16[4,272,512]{2,1,0:T(8,128)(2,1)}, u32[]{:S(2)}, u32[]{:S(2)}) collective-permute-start(bf16[4,272,512]{2,1,0:T(8,128)(2,1)} %get-tuple-element.45), channel_id=1, source_target_pairs={{1,2},{2,1},{5,6},{6,5},{9,10},{10,9},{13,14},{14,13},{17,18},{18,... | collective-permute-start | bytes 3342344 | tf_op jit(solution)/shard_map/ppermute | solution.py:149
  62.9 25.5 %collective-permute-start.3 = (bf16[2,512,512]{2,1,0:T(8,128)(2,1)}, bf16[2,512,512]{2,1,0:T(8,128)(2,1)}, u32[]{:S(2)}, u32[]{:S(2)}) collective-permute-start(bf16[2,512,512]{2,1,0:T(8,128)(2,1)} %get-tuple-element.41), channel_id=1, source_target_pairs={{8,0},{12,4},{16,8},{20,12},{24,16},{28,20},{9,1},{13,5},{17,9},{2... | collective-permute-start | bytes 3145736 | tf_op jit(solution)/shard_map/ppermute | solution.py:176
  65.8 34.9 %copy-start.15 = (bf16[2,512,512]{2,1,0:T(8,128)(2,1)S(1)}, bf16[2,512,512]{2,1,0:T(8,128)(2,1)}, u32[]{:S(2)}) copy-start(bf16[2,512,512]{2,1,0:T(8,128)(2,1)} %copy-done.14) | copy-start | bytes 3145732
  66.1 34.6 %copy-start.1 = (bf16[8,512,512]{2,1,0:T(8,128)(2,1)S(1)}, bf16[8,512,512]{2,1,0:T(8,128)(2,1)}, u32[]{:S(2)}) copy-start(bf16[8,512,512]{2,1,0:T(8,128)(2,1)} %copy-done) | copy-start | bytes 12582916
  125.7 111.5 %collective-permute-start.8 = (bf16[8,784,512]{2,1,0:T(8,128)(2,1)}, bf16[8,784,512]{2,1,0:T(8,128)(2,1)}, u32[]{:S(2)}, u32[]{:S(2)}) collective-permute-start(bf16[8,784,512]{2,1,0:T(8,128)(2,1)} %shard_map.37), channel_id=1, source_target_pairs={{0,4},{4,0},{8,12},{12,8},{16,20},{20,16},{24,28},{28,24},{1,5},{5... | collective-permute-start | bytes 19267592 | tf_op jit(solution)/shard_map/ppermute | solution.py:148
  129.8 6.0 %collective-permute-start.14 = (bf16[4,272,512]{2,1,0:T(8,128)(2,1)S(1)}, bf16[4,272,512]{2,1,0:T(8,128)(2,1)}, u32[]{:S(2)}, u32[]{:S(2)}) collective-permute-start(bf16[4,272,512]{2,1,0:T(8,128)(2,1)S(1)} %collective-permute-done.5), channel_id=1, source_target_pairs={{1,2},{2,1},{5,6},{6,5},{9,10},{10,9},{13,14},{14,13},{17,18},{18,... | collective-permute-start | bytes 3342344 | tf_op jit(solution)/shard_map/ppermute | solution.py:149
  131.5 5.7 %collective-permute-start.12 = (bf16[4,272,512]{2,1,0:T(8,128)(2,1)S(1)}, bf16[4,272,512]{2,1,0:T(8,128)(2,1)}, u32[]{:S(2)}, u32[]{:S(2)}) collective-permute-start(bf16[4,272,512]{2,1,0:T(8,128)(2,1)S(1)} %collective-permute-done.4), channel_id=1, source_target_pairs={{1,2},{2,1},{5,6},{6,5},{9,10},{10,9},{13,14},{14,13},{17,18},{18,... | collective-permute-start | bytes 3342344 | tf_op jit(solution)/shard_map/ppermute | solution.py:149
  133.1 31.4 %collective-permute-start.11 = (bf16[4,272,512]{2,1,0:T(8,128)(2,1)}, bf16[4,272,512]{2,1,0:T(8,128)(2,1)}, u32[]{:S(2)}, u32[]{:S(2)}) collective-permute-start(bf16[4,272,512]{2,1,0:T(8,128)(2,1)} %collective-permute-done.7), channel_id=1, source_target_pairs={{1,0},{2,3},{5,4},{6,7},{9,8},{10,11},{13,12},{14,15},{17,16},{18,... | collective-permute-start | bytes 3342344 | tf_op jit(solution)/shard_map/ppermute | solution.py:149
  134.4 59.5 %collective-permute-start.10 = (bf16[4,272,512]{2,1,0:T(8,128)(2,1)}, bf16[4,272,512]{2,1,0:T(8,128)(2,1)}, u32[]{:S(2)}, u32[]{:S(2)}) collective-permute-start(bf16[4,272,512]{2,1,0:T(8,128)(2,1)} %collective-permute-done.6), channel_id=1, source_target_pairs={{1,0},{2,3},{5,4},{6,7},{9,8},{10,11},{13,12},{14,15},{17,16},{18,... | collective-permute-start | bytes 3342344 | tf_op jit(solution)/shard_map/ppermute | solution.py:149
  135.8 76.4 %collective-permute-start.15 = (bf16[4,272,512]{2,1,0:T(8,128)(2,1)}, bf16[4,272,512]{2,1,0:T(8,128)(2,1)S(1)}, u32[]{:S(2)}, u32[]{:S(2)}) collective-permute-start(bf16[4,272,512]{2,1,0:T(8,128)(2,1)} %collective-permute-done.14), channel_id=1, source_target_pairs={{1,0},{2,3},{5,4},{6,7},{9,8},{10,11},{13,12},{14,15},{17,16},{18,... | collective-permute-start | bytes 3342344 | tf_op jit(solution)/shard_map/ppermute | solution.py:149
  137.2 98.9 %collective-permute-start.13 = (bf16[4,272,512]{2,1,0:T(8,128)(2,1)}, bf16[4,272,512]{2,1,0:T(8,128)(2,1)S(1)}, u32[]{:S(2)}, u32[]{:S(2)}) collective-permute-start(bf16[4,272,512]{2,1,0:T(8,128)(2,1)} %collective-permute-done.12), channel_id=1, source_target_pairs={{1,0},{2,3},{5,4},{6,7},{9,8},{10,11},{13,12},{14,15},{17,16},{18,... | collective-permute-start | bytes 3342344 | tf_op jit(solution)/shard_map/ppermute | solution.py:149
  138.6 98.6 %slice-start = ((s8[6422528]{0:T(1024)(128)(4,1)}), s8[4194304]{0:T(1024)(128)(4,1)S(1)}, s32[]{:S(2)}) async-start(s8[6422528]{0:T(1024)(128)(4,1)} %bitcast.118), calls=%async_computation | async-start | bytes 8388608
  164.6 103.8 %collective-permute-start.9 = (bf16[8,240,512]{2,1,0:T(8,128)(2,1)}, bf16[8,240,512]{2,1,0:T(8,128)(2,1)}, u32[]{:S(2)}, u32[]{:S(2)}) collective-permute-start(bf16[8,240,512]{2,1,0:T(8,128)(2,1)} %slice_select_fusion.1), channel_id=1, source_target_pairs={{0,1},{3,2},{4,5},{7,6},{8,9},{11,10},{12,13},{15,14},{16,17},{19,... | collective-permute-start | bytes 5898248 | tf_op jit(solution)/shard_map/ppermute | solution.py:149
  194.0 43.3 %slice-start.1 = ((s8[6422528]{0:T(1024)(128)(4,1)}), s8[2228224]{0:T(1024)(128)(4,1)S(1)}, s32[]{:S(2)}) async-start(s8[6422528]{0:T(1024)(128)(4,1)} %bitcast.118), calls=%async_computation.1 | async-start | bytes 4456448
  277.4 17.4 %copy-start.11 = (f32[1024,512]{0,1:T(8,128)}, f32[1024,512]{0,1:T(8,128)S(1)}, u32[]{:S(2)}) copy-start(f32[1024,512]{0,1:T(8,128)S(1)} %fusion.29) | copy-start | bytes 6291460
  279.4 15.4 %copy-start.13 = (bf16[4,272,512]{2,1,0:T(8,128)(2,1)S(1)}, bf16[4,272,512]{2,1,0:T(8,128)(2,1)}, u32[]{:S(2)}) copy-start(bf16[4,272,512]{2,1,0:T(8,128)(2,1)} %broadcast_select_fusion.1) | copy-start | bytes 3342340
  321.3 12.6 %collective-permute-start.16 = (bf16[512,512]{0,1:T(8,128)(2,1)}, bf16[512,512]{0,1:T(8,128)(2,1)}, u32[]{:S(2)}, u32[]{:S(2)}) collective-permute-start(bf16[512,512]{0,1:T(8,128)(2,1)} %get-tuple-element.48), channel_id=1, source_target_pairs={{0,16},{4,20},{8,24},{12,28},{16,0},{20,4},{24,8},{28,12},{1,17},{... | collective-permute-start | bytes 1572872 | tf_op jit(solution)/shard_map/ppermute | solution.py:148
  321.3 23.9 %collective-permute-start.17 = (bf16[512,512]{0,1:T(8,128)(2,1)}, bf16[512,512]{0,1:T(8,128)(2,1)}, u32[]{:S(2)}, u32[]{:S(2)}) collective-permute-start(bf16[512,512]{0,1:T(8,128)(2,1)} %get-tuple-element.50), channel_id=1, source_target_pairs={{0,16},{4,20},{8,24},{12,28},{16,0},{20,4},{24,8},{28,12},{1,17},{... | collective-permute-start | bytes 1572872 | tf_op jit(solution)/shard_map/ppermute | solution.py:148
  322.8 22.4 %collective-permute-start.19 = (bf16[512,512]{0,1:T(8,128)(2,1)}, bf16[512,512]{0,1:T(8,128)(2,1)}, u32[]{:S(2)}, u32[]{:S(2)}) collective-permute-start(bf16[512,512]{0,1:T(8,128)(2,1)} %get-tuple-element.49), channel_id=1, source_target_pairs={{0,8},{4,12},{8,0},{12,4},{16,24},{20,28},{24,16},{28,20},{1,9},{5... | collective-permute-start | bytes 1572872 | tf_op jit(solution)/shard_map/ppermute | solution.py:148
  327.2 28.0 %collective-permute-start.20 = (bf16[512,512]{1,0:T(8,128)(2,1)}, bf16[512,512]{1,0:T(8,128)(2,1)}, u32[]{:S(2)}, u32[]{:S(2)}) collective-permute-start(bf16[512,512]{1,0:T(8,128)(2,1)} %select_convert_fusion.1), channel_id=1, source_target_pairs={{0,8},{4,12},{8,0},{12,4},{16,24},{20,28},{24,16},{28,20},{1,9},{5... | collective-permute-start | bytes 1572872 | tf_op jit(solution)/shard_map/ppermute | solution.py:148
  357.9 11.7 %collective-permute-start.21 = (bf16[512,512]{1,0:T(8,128)(2,1)}, bf16[512,512]{1,0:T(8,128)(2,1)}, u32[]{:S(2)}, u32[]{:S(2)}) collective-permute-start(bf16[512,512]{1,0:T(8,128)(2,1)} %get-tuple-element.27), channel_id=1, source_target_pairs={{0,16},{4,20},{8,24},{12,28},{16,0},{20,4},{24,8},{28,12},{1,17},{... | collective-permute-start | bytes 1572872 | tf_op jit(solution)/shard_map/ppermute | solution.py:148
  360.9 13.4 %collective-permute-start.18 = (bf16[512,512]{0,1:T(8,128)(2,1)}, bf16[512,512]{0,1:T(8,128)(2,1)}, u32[]{:S(2)}, u32[]{:S(2)}) collective-permute-start(bf16[512,512]{0,1:T(8,128)(2,1)} %get-tuple-element.39), channel_id=1, source_target_pairs={{0,8},{4,12},{8,0},{12,4},{16,24},{20,28},{24,16},{28,20},{1,9},{5... | collective-permute-start | bytes 1572872 | tf_op jit(solution)/shard_map/ppermute | solution.py:148
  379.1 63.2 %collective-permute-start.23 = (bf16[512,512]{0,1:T(8,128)(2,1)}, bf16[512,512]{0,1:T(8,128)(2,1)}, u32[]{:S(2)}, u32[]{:S(2)}) collective-permute-start(bf16[512,512]{0,1:T(8,128)(2,1)} %broadcast_select_fusion.10), channel_id=1, source_target_pairs={{1,12},{2,20},{3,28},{5,8},{6,16},{7,24},{8,5},{10,21},{11,29},{12... | collective-permute-start | bytes 1572872 | tf_op jit(solution)/shard_map/ppermute | solution.py:296
  384.5 69.0 %collective-permute-start.22 = (bf16[512,512]{0,1:T(8,128)(2,1)}, bf16[512,512]{0,1:T(8,128)(2,1)}, u32[]{:S(2)}, u32[]{:S(2)}) collective-permute-start(bf16[512,512]{0,1:T(8,128)(2,1)} %get-tuple-element.25), channel_id=1, source_target_pairs={{1,8},{2,16},{3,24},{5,12},{6,20},{7,28},{8,1},{10,17},{11,25},{12... | collective-permute-start | bytes 1572872 | tf_op jit(solution)/shard_map/ppermute | solution.py:295
  388.1 65.4 %copy-start.6 = (f32[512,512]{1,0:T(8,128)S(1)}, f32[512,512]{1,0:T(8,128)}, u32[]{:S(2)}) copy-start(f32[512,512]{1,0:T(8,128)} %convert_add_fusion) | copy-start | bytes 3145732
  (14 other events, 72.7 us)

commit v3 on v2

--- a/solution.py
+++ b/solution.py
@@ -202,7 +202,6 @@
     out_inner = [along(p, P_OUT) for p in cross_a]
     cross_outer = [along(p, P_CROSS) for p in in_a]
     in_b = along(part_b, P_IN)
-    out_outer = [along(p, P_OUT) for p in cross_outer]
     pair_norm = pair_sum(code_all, rows * spots, cols)
 
     band = 2 * rows
@@ -243,6 +242,10 @@
         mat = jnp.where(col_same, mat, 0.0)
         mats.append(jnp.concatenate([mat, cut(mat) * share]).astype(jnp.bfloat16))
     lag = lag_call(row_same, z_wide, jnp.stack(mats))
+    lag, out_inner[0], cross_outer[0] = lax.optimization_barrier(
+        (lag, out_inner[0], cross_outer[0])
+    )
+    out_outer = [along(p, P_OUT) for p in cross_outer]
     lag_taken = swap(lag, 1)
     lag_both = ordered(first, lag, lag_taken, 2)
     flat = lambda a: a.reshape(-1, a.shape[-1])

time: 461 us -> 440 us (0.954)
  starting transfers between devices: 66.6 us -> 49.8 us
  waiting for transfers between devices: 179 us -> 174 us
    ppermute x11, starting transfers between devices: 43.9 us -> 27 us  [mirrored_shards(): along = lambda a, perm: lax.ppermute(a, 'gene', perm)]
    unnamed x47 -> x55, local copies, waits for them, and re-layouts: 8.79 us -> 9.86 us
  transfers between devices with their start and end apart: 24 -> 24, of which waited for: 11 -> 11; matrix products, arithmetic and copies ran while one was open for 16% -> 17% of each run, Pallas kernels for 0% -> 5%
where the time goes in v3:
time: 440 us; the launch traced here: 435 us
  waiting for transfers between devices  174 us (40%)
  other arithmetic  68.5 us (16%)
  starting transfers between devices  49.8 us (11%)
  matrix products  45.9 us (10%)
  local copies, waits for them, and re-layouts  45 us (10%)
  blocking collectives  28.2 us (6%)
  Pallas kernels  21.3 us (5%)
    ppermute x11, waiting for transfers between devices, mirrored_shards(): along = lambda a, perm: lax.ppermute(a, 'gene', perm)  71.1 us
    ppermute x1, waiting for transfers between devices, mirrored_shards(): lax.ppermute(jnp.where(first, bottom_n, top_n), ('spot', 'gene'), other_c...  51.9 us
    dot_general x6, matrix products, cross_panel(): lax.dot_general(left, right, contract_bins, preferred_element_type=jnp.fl...  45.9 us
    ppermute x11, starting transfers between devices, mirrored_shards(): along = lambda a, perm: lax.ppermute(a, 'gene', perm)  27 us
    ppermute x1, waiting for transfers between devices, mirrored_shards(): below = lax.ppermute(dev[:2], 'spot', [(i + 2, i) for i in range(steps)])  22.1 us
    pallas_call x1, Pallas kernels, lag_call(): pl.pallas_call(lag_kernel, out_shape=jax.ShapeDtypeStruct((rows, tall, ge...  21.3 us
    ppermute x9, waiting for transfers between devices, mirrored_shards(): lax.ppermute(a, 'spot', [(i, i ^ bit) for i in range(spots)])  17 us
    convert_element_type x4, other arithmetic, mirrored_shards(): narrow = lambda a: a.astype(jnp.bfloat16)  14 us
  transfers between devices with their start and end apart: 24, of which 11 were waited for; matrix products, arithmetic and copies ran while one was open for 17% of the time, Pallas kernels for 5%

profile of v3, /device:TPU:3, one launch (start us, length us, event | category | flops | bytes accessed | tf_op | source)
XLA Modules:
  0.0 435.4 jit_solution(9053296611254203522)
XLA Ops:
  0.0 3.9 multiply_convert_fusion.1
  6.6 9.5 %all-gather.2 = s32[8,4,512]{2,1,0:T(4,128)S(1)} all-gather(s32[1,4,512]{2,1,0:T(4,128)S(1)} %bitcast.121), channel_id=1, replica_groups=mesh['spot'=8,'gene'=4] {'spot'}, dimensions={0}, use_global_device_ids=true | all-gather | bytes 73728 | tf_op jit(solution)/shard_map/all_gather | solution.py:178
  21.5 4.4 %convert_reduce_fusion = (f32[512]{0:T(512)S(1)}, f32[512]{0:T(512)S(1)}, bf16[8,512,512]{2,1,0:T(8,128)(2,1)S(1)}) fusion(f32[512]{0:T(512)S(1)} %divide_round-nearest-even_fusion, f32[8,512]{1,0:T(8,128)S(1)} %get-tuple-element.38, bf16[4,512,512]{2,1,0:T(8,128)(2,1)S(1)} %get-tuple-element.50, bf16[4,512,512]{2,1,0:T(8,128)(2,1)} %collective-permute-done, ...), kind=kLoop, calls=%fused_computation.3 | loop fusion | flops 23067648 | bytes 8411137 | tf_op jit(solution)/shard_map/reduce_sum | solution.py:182
  26.0 8.2 %all-gather.3 = f32[8,4,512]{2,1,0:T(4,128)S(1)} all-gather(f32[1,4,512]{2,1,0:T(4,128)S(1)} %maximum_bitcast_fusion), channel_id=2, replica_groups=mesh['spot'=8,'gene'=4] {'spot'}, dimensions={0}, use_global_device_ids=true | all-gather | bytes 73728 | tf_op jit(solution)/shard_map/all_gather | solution.py:188
  35.5 3.1 collective-permute-start.2
  38.6 10.5 %all-gather.4 = f32[4,2,512]{2,1,0:T(2,128)S(1)} all-gather(f32[1,2,512]{2,1,0:T(2,128)S(1)} %maximum_bitcast_fusion.1), channel_id=3, replica_groups=mesh['spot'=8,'gene'=4] {'gene'}, dimensions={0}, use_global_device_ids=true | all-gather | bytes 20480 | tf_op jit(solution)/shard_map/all_gather | solution.py:196
  52.4 3.5 collective-permute-start.4
  66.4 22.1 %collective-permute-done.3 = bf16[2,512,512]{2,1,0:T(8,128)(2,1)} collective-permute-done((bf16[2,512,512]{2,1,0:T(8,128)(2,1)}, bf16[2,512,512]{2,1,0:T(8,128)(2,1)}, u32[]{:S(2)}, u32[]{:S(2)}) %collective-permute-start.3) | collective-permute-done | bytes 1048608 | tf_op jit(solution)/shard_map/ppermute | solution.py:176
  88.4 12.2 %collective-permute-done.5 = bf16[4,272,512]{2,1,0:T(8,128)(2,1)S(1)} collective-permute-done((bf16[4,272,512]{2,1,0:T(8,128)(2,1)}, bf16[4,272,512]{2,1,0:T(8,128)(2,1)S(1)}, u32[]{:S(2)}, u32[]{:S(2)}) %collective-permute-start.5) | collective-permute-done | bytes 1114144 | tf_op jit(solution)/shard_map/ppermute | solution.py:149
  102.7 3.7 multiply_convert_fusion.z_ref
  106.5 21.3 %shard_map.37 = bf16[8,784,512]{2,1,0:T(8,128)(2,1)} custom-call(f32[8,5]{1,0:T(8,128)S(1)} %stack.57.row_same, bf16[12,512,512]{2,1,0:T(8,128)(2,1)S(1)} %multiply_convert_fusion.z_ref, bf16[3,784,512]{2,1,0:T(8,128)(2,1)S(1)} %maximum_maximum_fusion.mat_ref), custom_call_target="tpu_custom_call" | custom-call | flops 16441671680 | bytes 12582912 | tf_op jit(solution)/shard_map/pallas_call | solution.py:111
  128.8 4.1 collective-permute-start.10
  137.3 11.0 %collective-permute-start.11 = (bf16[8,240,512]{2,1,0:T(8,128)(2,1)}, bf16[8,240,512]{2,1,0:T(8,128)(2,1)}, u32[]{:S(2)}, u32[]{:S(2)}) collective-permute-start(bf16[8,240,512]{2,1,0:T(8,128)(2,1)} %slice_select_fusion.1), channel_id=1, source_target_pairs={{0,1},{3,2},{4,5},{7,6},{8,9},{11,10},{12,13},{15,14},{16,17},{19,... | collective-permute-start | bytes 5898248 | tf_op jit(solution)/shard_map/ppermute | solution.py:149
  152.4 14.8 %collective-permute-done.12 = bf16[4,272,512]{2,1,0:T(8,128)(2,1)} collective-permute-done((bf16[4,272,512]{2,1,0:T(8,128)(2,1)}, bf16[4,272,512]{2,1,0:T(8,128)(2,1)}, u32[]{:S(2)}, u32[]{:S(2)}) %collective-permute-start.12) | collective-permute-done | bytes 1114144 | tf_op jit(solution)/shard_map/ppermute | solution.py:149
  169.7 21.3 %collective-permute-done.13 = bf16[4,272,512]{2,1,0:T(8,128)(2,1)S(1)} collective-permute-done((bf16[4,272,512]{2,1,0:T(8,128)(2,1)}, bf16[4,272,512]{2,1,0:T(8,128)(2,1)S(1)}, u32[]{:S(2)}, u32[]{:S(2)}) %collective-permute-start.13) | collective-permute-done | bytes 1114144 | tf_op jit(solution)/shard_map/ppermute | solution.py:149
  192.1 22.8 %collective-permute-done.15 = bf16[4,272,512]{2,1,0:T(8,128)(2,1)S(1)} collective-permute-done((bf16[4,272,512]{2,1,0:T(8,128)(2,1)}, bf16[4,272,512]{2,1,0:T(8,128)(2,1)S(1)}, u32[]{:S(2)}, u32[]{:S(2)}) %collective-permute-start.15) | collective-permute-done | bytes 1114144 | tf_op jit(solution)/shard_map/ppermute | solution.py:149
  216.0 8.4 %maximum_select_fusion = bf16[8,784,1024]{2,1,0:T(8,128)(2,1)S(1)} fusion(bf16[8,784,512]{2,1,0:T(8,128)(2,1)} %collective-permute-done.10, bf16[8,784,512]{2,1,0:T(8,128)(2,1)S(1)} %bitcast.119, pred[]{:T(512)S(6)} %eq.239), kind=kLoop, calls=%fused_computation | loop fusion | flops 57802752 | bytes 25690112 | tf_op jit(solution)/shard_map/jit(_where)/select_n | solution.py:150
  224.5 4.6 %copy-done.2 = bf16[8,784,1024]{2,1,0:T(8,128)(2,1)} copy-done((bf16[8,784,1024]{2,1,0:T(8,128)(2,1)}, bf16[8,784,1024]{2,1,0:T(8,128)(2,1)S(1)}, u32[]{:S(2)}) %copy-start.2) | copy-done | bytes 12845080
  232.3 9.7 %fusion.30 = f32[1024,512]{1,0:T(8,128)S(1)} fusion(f32[1024,512]{1,0:T(8,128)} %copy.168, bf16[8,512,512]{2,1,0:T(8,128)(2,1)} %copy-done, bf16[8,784,1024]{2,1,0:T(8,128)(2,1)} %copy-done.2, f32[512]{0:T(512)S(1)} %bitcast.140), kind=kOutput, calls=%fused_computation.46 | convolution fusion | flops 4296015872 | bytes 16779264 | tf_op jit(solution)/shard_map/dot_general | solution.py:35
  244.0 3.1 fusion.16
  247.1 9.0 %fusion.29 = f32[1024,512]{0,1:T(8,128)S(1)} fusion(bf16[8,240,512]{2,1,0:T(8,128)(2,1)} %collective-permute-done.11, bf16[8,272,512]{2,1,0:T(8,128)(2,1)S(1)} %copy-done.21, pred[]{:T(512)S(6)} %lt.66, bf16[8,784,1024]{2,1,0:T(8,128)(2,1)} %copy-done.2, f32[512]{0:T(512)S(1)} %bitcast.139, f32[512]{0:T(512)S(1)} %bitcast.138, f32[1024]{0:T(1024)S(1)} %bitcast.133, ...), kind=kOutput, calls=%fused_computation.44 | convolution fusion | flops 4315938816 | bytes 14688258 | tf_op jit(solution)/shard_map/dot_general | solution.py:35
  258.2 15.4 %fusion.18 = f32[1024,512,1]{0,1,2:T(8,128)S(1)} fusion(bf16[8,784,1024]{2,1,0:T(8,128)(2,1)} %copy-done.2, bf16[4,272,512]{2,1,0:T(8,128)(2,1)} %broadcast_select_fusion.2, bf16[4,272,512]{2,1,0:T(8,128)(2,1)} %broadcast_select_fusion.3), kind=kOutput, calls=%fused_computation.27 | convolution fusion | flops 2282815488 | bytes 8781824 | tf_op jit(solution)/shard_map/dot_general | solution.py:35
  273.6 7.5 %broadcast_select_fusion.8 = (f32[1024,512]{0,1:T(8,128)}, f32[1024,512]{0,1:T(8,128)}, f32[1024,512]{0,1:T(8,128)S(1)}) fusion(pred[]{:T(512)S(6)} %lt.66, f32[1024,512]{0,1:T(8,128)S(1)} %copy-done.10, f32[1024,512]{0,1:T(8,128)} %copy-done.11, pred[]{:T(512)S(6)} %eq.238, f32[512]{0:T(512)S(1)} %bitcast.136, f32[512]{0:T(512)S(1)} %bitcast.134, ...), kind=kOutput, calls=%fused_computation.82 | convolution fusion | flops 2288582656 | bytes 19279874 | tf_op jit(solution)/shard_map/dot_general | solution.py:35
  283.1 5.0 %broadcast_select_fusion.4 = (f32[1024,512]{1,0:T(8,128)}, f32[1024,512]{1,0:T(8,128)}) fusion(f32[1024,512]{1,0:T(8,128)} %copy.178, pred[]{:T(512)S(6)} %lt.66, f32[1024,512]{1,0:T(8,128)} %copy.175, f32[1024,512]{1,0:T(8,128)} %copy-done.8, pred[]{:T(512)S(6)} %eq.238), kind=kLoop, calls=%fused_computation.78 | loop fusion | flops 1048576 | bytes 10485762 | tf_op jit(solution)/shard_map/jit(_where)/select_n | solution.py:277
  296.2 3.8 select_convert_fusion.5
  312.6 11.2 %collective-permute-done.17 = bf16[512,512]{0,1:T(8,128)(2,1)} collective-permute-done((bf16[512,512]{0,1:T(8,128)(2,1)}, bf16[512,512]{0,1:T(8,128)(2,1)}, u32[]{:S(2)}, u32[]{:S(2)}) %collective-permute-start.17) | collective-permute-done | bytes 524320 | tf_op jit(solution)/shard_map/ppermute | solution.py:148
  323.9 5.2 %select_convert_fusion.3 = (bf16[512,512]{0,1:T(8,128)(2,1)}, f32[512,512]{0,1:T(8,128)}, f32[512,512]{0,1:T(8,128)}) fusion(pred[]{:T(512)S(6)} %eq.236, bf16[512,512]{0,1:T(8,128)(2,1)} %collective-permute-done.17, f32[512,512]{0,1:T(8,128)S(1)} %copy.204, f32[1024,512]{0,1:T(8,128)S(1)} %broadcast_select_fusion.7, pred[]{:T(512)S(6)} %eq.237, ...), kind=kLoop, calls=%fused_computation.68 | loop fusion | flops 3145728 | bytes 12582914 | tf_op jit(solution)/shard_map/convert_element_type | solution.py:279
  353.0 3.7 broadcast_select_fusion.11
  357.7 5.5 %collective-permute-start.23 = (bf16[512,512]{0,1:T(8,128)(2,1)}, bf16[512,512]{0,1:T(8,128)(2,1)}, u32[]{:S(2)}, u32[]{:S(2)}) collective-permute-start(bf16[512,512]{0,1:T(8,128)(2,1)} %broadcast_select_fusion.10), channel_id=1, source_target_pairs={{1,12},{2,20},{3,28},{5,8},{6,16},{7,24},{8,5},{10,21},{11,29},{12... | collective-permute-start | bytes 1572872 | tf_op jit(solution)/shard_map/ppermute | solution.py:299
  363.2 3.4 collective-permute-start.22
  369.0 51.9 %collective-permute-done.23 = bf16[512,512]{0,1:T(8,128)(2,1)} collective-permute-done((bf16[512,512]{0,1:T(8,128)(2,1)}, bf16[512,512]{0,1:T(8,128)(2,1)}, u32[]{:S(2)}, u32[]{:S(2)}) %collective-permute-start.23) | collective-permute-done | bytes 524320 | tf_op jit(solution)/shard_map/ppermute | solution.py:299
  420.9 11.2 %collective-permute-done.22 = bf16[512,512]{0,1:T(8,128)(2,1)} collective-permute-done((bf16[512,512]{0,1:T(8,128)(2,1)}, bf16[512,512]{0,1:T(8,128)(2,1)}, u32[]{:S(2)}, u32[]{:S(2)}) %collective-permute-start.22) | collective-permute-done | bytes 524320 | tf_op jit(solution)/shard_map/ppermute | solution.py:298
  (164 shorter events, 98.1 us)
Async XLA Ops:
  5.8 12.8 %collective-permute-start = (bf16[4,512,512]{2,1,0:T(8,128)(2,1)}, bf16[4,512,512]{2,1,0:T(8,128)(2,1)}, u32[]{:S(2)}, u32[]{:S(2)}) collective-permute-start(bf16[4,512,512]{2,1,0:T(8,128)(2,1)} %get-tuple-element.49), channel_id=1, source_target_pairs={{0,4},{4,0},{8,12},{12,8},{16,20},{20,16},{24,28},{28,24},{1,5},{5... | collective-permute-start | bytes 6291464 | tf_op jit(solution)/shard_map/ppermute | solution.py:148
  6.5 10.0 %collective-permute-start.1 = (s32[4,512]{1,0:T(4,128)S(1)}, s32[4,512]{1,0:T(4,128)S(1)}, u32[]{:S(2)}, u32[]{:S(2)}) collective-permute-start(s32[4,512]{1,0:T(4,128)S(1)} %multiply_add_fusion), channel_id=1, source_target_pairs={{0,4},{4,0},{8,12},{12,8},{16,20},{20,16},{24,28},{28,24},{1,5},{5... | collective-permute-start | bytes 24584 | tf_op jit(solution)/shard_map/ppermute | solution.py:148
  25.9 24.7 %copy-start = (bf16[8,512,512]{2,1,0:T(8,128)(2,1)}, bf16[8,512,512]{2,1,0:T(8,128)(2,1)S(1)}, u32[]{:S(2)}) copy-start(bf16[8,512,512]{2,1,0:T(8,128)(2,1)S(1)} %get-tuple-element.41) | copy-start | bytes 12582916
  35.5 26.5 %collective-permute-start.2 = (bf16[2,512,512]{2,1,0:T(8,128)(2,1)S(1)}, bf16[2,512,512]{2,1,0:T(8,128)(2,1)S(1)}, u32[]{:S(2)}, u32[]{:S(2)}) collective-permute-start(bf16[2,512,512]{2,1,0:T(8,128)(2,1)S(1)} %get-tuple-element.48), channel_id=1, source_target_pairs={{0,8},{4,12},{8,16},{12,20},{16,24},{20,28},{1,9},{5,13},{9,17},{1... | collective-permute-start | bytes 3145736 | tf_op jit(solution)/shard_map/ppermute | solution.py:175
  52.4 36.1 %collective-permute-start.4 = (bf16[4,272,512]{2,1,0:T(8,128)(2,1)}, bf16[4,272,512]{2,1,0:T(8,128)(2,1)S(1)}, u32[]{:S(2)}, u32[]{:S(2)}) collective-permute-start(bf16[4,272,512]{2,1,0:T(8,128)(2,1)} %get-tuple-element.52), channel_id=1, source_target_pairs={{0,1},{3,2},{4,5},{7,6},{8,9},{11,10},{12,13},{15,14},{16,17},{19,... | collective-permute-start | bytes 3342344 | tf_op jit(solution)/shard_map/ppermute | solution.py:149
  55.9 44.8 %collective-permute-start.6 = (bf16[4,272,512]{2,1,0:T(8,128)(2,1)}, bf16[4,272,512]{2,1,0:T(8,128)(2,1)}, u32[]{:S(2)}, u32[]{:S(2)}) collective-permute-start(bf16[4,272,512]{2,1,0:T(8,128)(2,1)} %get-tuple-element.52), channel_id=1, source_target_pairs={{1,2},{2,1},{5,6},{6,5},{9,10},{10,9},{13,14},{14,13},{17,18},{18,... | collective-permute-start | bytes 3342344 | tf_op jit(solution)/shard_map/ppermute | solution.py:149
  57.6 43.0 %collective-permute-start.5 = (bf16[4,272,512]{2,1,0:T(8,128)(2,1)}, bf16[4,272,512]{2,1,0:T(8,128)(2,1)S(1)}, u32[]{:S(2)}, u32[]{:S(2)}) collective-permute-start(bf16[4,272,512]{2,1,0:T(8,128)(2,1)} %get-tuple-element.51), channel_id=1, source_target_pairs={{0,1},{3,2},{4,5},{7,6},{8,9},{11,10},{12,13},{15,14},{16,17},{19,... | collective-permute-start | bytes 3342344 | tf_op jit(solution)/shard_map/ppermute | solution.py:149
  59.1 41.6 %collective-permute-start.7 = (bf16[4,272,512]{2,1,0:T(8,128)(2,1)}, bf16[4,272,512]{2,1,0:T(8,128)(2,1)}, u32[]{:S(2)}, u32[]{:S(2)}) collective-permute-start(bf16[4,272,512]{2,1,0:T(8,128)(2,1)} %get-tuple-element.51), channel_id=1, source_target_pairs={{1,2},{2,1},{5,6},{6,5},{9,10},{10,9},{13,14},{14,13},{17,18},{18,... | collective-permute-start | bytes 3342344 | tf_op jit(solution)/shard_map/ppermute | solution.py:149
  62.9 25.5 %collective-permute-start.3 = (bf16[2,512,512]{2,1,0:T(8,128)(2,1)}, bf16[2,512,512]{2,1,0:T(8,128)(2,1)}, u32[]{:S(2)}, u32[]{:S(2)}) collective-permute-start(bf16[2,512,512]{2,1,0:T(8,128)(2,1)} %get-tuple-element.47), channel_id=1, source_target_pairs={{8,0},{12,4},{16,8},{20,12},{24,16},{28,20},{9,1},{13,5},{17,9},{2... | collective-permute-start | bytes 3145736 | tf_op jit(solution)/shard_map/ppermute | solution.py:176
  65.8 36.9 %copy-start.19 = (bf16[2,512,512]{2,1,0:T(8,128)(2,1)S(1)}, bf16[2,512,512]{2,1,0:T(8,128)(2,1)}, u32[]{:S(2)}) copy-start(bf16[2,512,512]{2,1,0:T(8,128)(2,1)} %copy-done.18) | copy-start | bytes 3145732
  66.1 36.7 %copy-start.1 = (bf16[8,512,512]{2,1,0:T(8,128)(2,1)S(1)}, bf16[8,512,512]{2,1,0:T(8,128)(2,1)}, u32[]{:S(2)}) copy-start(bf16[8,512,512]{2,1,0:T(8,128)(2,1)} %copy-done) | copy-start | bytes 12582916
  100.7 27.1 %collective-permute-start.8 = (bf16[4,272,512]{2,1,0:T(8,128)(2,1)}, bf16[4,272,512]{2,1,0:T(8,128)(2,1)S(1)}, u32[]{:S(2)}, u32[]{:S(2)}) collective-permute-start(bf16[4,272,512]{2,1,0:T(8,128)(2,1)} %collective-permute-done.6), channel_id=1, source_target_pairs={{1,0},{2,3},{5,4},{6,7},{9,8},{10,11},{13,12},{14,15},{17,16},{18,... | collective-permute-start | bytes 3342344 | tf_op jit(solution)/shard_map/ppermute | solution.py:149
  102.0 25.8 %collective-permute-start.9 = (bf16[4,272,512]{2,1,0:T(8,128)(2,1)S(1)}, bf16[4,272,512]{2,1,0:T(8,128)(2,1)S(1)}, u32[]{:S(2)}, u32[]{:S(2)}) collective-permute-start(bf16[4,272,512]{2,1,0:T(8,128)(2,1)S(1)} %collective-permute-done.4), channel_id=1, source_target_pairs={{1,2},{2,1},{5,6},{6,5},{9,10},{10,9},{13,14},{14,13},{17,18},{18,... | collective-permute-start | bytes 3342344 | tf_op jit(solution)/shard_map/ppermute | solution.py:149
  128.8 87.2 %collective-permute-start.10 = (bf16[8,784,512]{2,1,0:T(8,128)(2,1)}, bf16[8,784,512]{2,1,0:T(8,128)(2,1)}, u32[]{:S(2)}, u32[]{:S(2)}) collective-permute-start(bf16[8,784,512]{2,1,0:T(8,128)(2,1)} %shard_map.37), channel_id=1, source_target_pairs={{0,4},{4,0},{8,12},{12,8},{16,20},{20,16},{24,28},{28,24},{1,5},{5... | collective-permute-start | bytes 19267592 | tf_op jit(solution)/shard_map/ppermute | solution.py:148
  132.9 15.4 %collective-permute-start.14 = (bf16[4,272,512]{2,1,0:T(8,128)(2,1)S(1)}, bf16[4,272,512]{2,1,0:T(8,128)(2,1)}, u32[]{:S(2)}, u32[]{:S(2)}) collective-permute-start(bf16[4,272,512]{2,1,0:T(8,128)(2,1)S(1)} %collective-permute-done.5), channel_id=1, source_target_pairs={{1,2},{2,1},{5,6},{6,5},{9,10},{10,9},{13,14},{14,13},{17,18},{18,... | collective-permute-start | bytes 3342344 | tf_op jit(solution)/shard_map/ppermute | solution.py:149
  134.5 32.7 %collective-permute-start.12 = (bf16[4,272,512]{2,1,0:T(8,128)(2,1)}, bf16[4,272,512]{2,1,0:T(8,128)(2,1)}, u32[]{:S(2)}, u32[]{:S(2)}) collective-permute-start(bf16[4,272,512]{2,1,0:T(8,128)(2,1)} %collective-permute-done.7), channel_id=1, source_target_pairs={{1,0},{2,3},{5,4},{6,7},{9,8},{10,11},{13,12},{14,15},{17,16},{18,... | collective-permute-start | bytes 3342344 | tf_op jit(solution)/shard_map/ppermute | solution.py:149
  135.9 55.1 %collective-permute-start.13 = (bf16[4,272,512]{2,1,0:T(8,128)(2,1)}, bf16[4,272,512]{2,1,0:T(8,128)(2,1)S(1)}, u32[]{:S(2)}, u32[]{:S(2)}) collective-permute-start(bf16[4,272,512]{2,1,0:T(8,128)(2,1)} %copy-done.12), channel_id=1, source_target_pairs={{1,0},{2,3},{5,4},{6,7},{9,8},{10,11},{13,12},{14,15},{17,16},{18,... | collective-permute-start | bytes 3342344 | tf_op jit(solution)/shard_map/ppermute | solution.py:149
  137.3 109.8 %collective-permute-start.11 = (bf16[8,240,512]{2,1,0:T(8,128)(2,1)}, bf16[8,240,512]{2,1,0:T(8,128)(2,1)}, u32[]{:S(2)}, u32[]{:S(2)}) collective-permute-start(bf16[8,240,512]{2,1,0:T(8,128)(2,1)} %slice_select_fusion.1), channel_id=1, source_target_pairs={{0,1},{3,2},{4,5},{7,6},{8,9},{11,10},{12,13},{15,14},{16,17},{19,... | collective-permute-start | bytes 5898248 | tf_op jit(solution)/shard_map/ppermute | solution.py:149
  148.3 66.6 %collective-permute-start.15 = (bf16[4,272,512]{2,1,0:T(8,128)(2,1)}, bf16[4,272,512]{2,1,0:T(8,128)(2,1)S(1)}, u32[]{:S(2)}, u32[]{:S(2)}) collective-permute-start(bf16[4,272,512]{2,1,0:T(8,128)(2,1)} %collective-permute-done.14), channel_id=1, source_target_pairs={{1,0},{2,3},{5,4},{6,7},{9,8},{10,11},{13,12},{14,15},{17,16},{18,... | collective-permute-start | bytes 3342344 | tf_op jit(solution)/shard_map/ppermute | solution.py:149
  149.8 66.1 %slice-start = ((s8[6422528]{0:T(1024)(128)(4,1)}), s8[4194304]{0:T(1024)(128)(4,1)S(1)}, s32[]{:S(2)}) async-start(s8[6422528]{0:T(1024)(128)(4,1)} %bitcast.118), calls=%async_computation | async-start | bytes 8388608
  152.4 38.6 %copy-start.13 = (bf16[4,272,512]{2,1,0:T(8,128)(2,1)S(1)}, bf16[4,272,512]{2,1,0:T(8,128)(2,1)}, u32[]{:S(2)}) copy-start(bf16[4,272,512]{2,1,0:T(8,128)(2,1)} %copy-done.12) | copy-start | bytes 3342340
  152.4 63.5 %slice-start.1 = ((s8[6422528]{0:T(1024)(128)(4,1)}), s8[2228224]{0:T(1024)(128)(4,1)S(1)}, s32[]{:S(2)}) async-start(s8[6422528]{0:T(1024)(128)(4,1)} %bitcast.118), calls=%async_computation.1 | async-start | bytes 4456448
  256.2 17.4 %copy-start.11 = (f32[1024,512]{0,1:T(8,128)}, f32[1024,512]{0,1:T(8,128)S(1)}, u32[]{:S(2)}) copy-start(f32[1024,512]{0,1:T(8,128)S(1)} %fusion.29) | copy-start | bytes 6291460
  300.1 12.6 %collective-permute-start.16 = (bf16[512,512]{0,1:T(8,128)(2,1)}, bf16[512,512]{0,1:T(8,128)(2,1)}, u32[]{:S(2)}, u32[]{:S(2)}) collective-permute-start(bf16[512,512]{0,1:T(8,128)(2,1)} %get-tuple-element.54), channel_id=1, source_target_pairs={{0,16},{4,20},{8,24},{12,28},{16,0},{20,4},{24,8},{28,12},{1,17},{... | collective-permute-start | bytes 1572872 | tf_op jit(solution)/shard_map/ppermute | solution.py:148
  300.1 23.8 %collective-permute-start.17 = (bf16[512,512]{0,1:T(8,128)(2,1)}, bf16[512,512]{0,1:T(8,128)(2,1)}, u32[]{:S(2)}, u32[]{:S(2)}) collective-permute-start(bf16[512,512]{0,1:T(8,128)(2,1)} %get-tuple-element.56), channel_id=1, source_target_pairs={{0,16},{4,20},{8,24},{12,28},{16,0},{20,4},{24,8},{28,12},{1,17},{... | collective-permute-start | bytes 1572872 | tf_op jit(solution)/shard_map/ppermute | solution.py:148
  301.5 22.4 %collective-permute-start.19 = (bf16[512,512]{0,1:T(8,128)(2,1)}, bf16[512,512]{0,1:T(8,128)(2,1)}, u32[]{:S(2)}, u32[]{:S(2)}) collective-permute-start(bf16[512,512]{0,1:T(8,128)(2,1)} %get-tuple-element.55), channel_id=1, source_target_pairs={{0,8},{4,12},{8,0},{12,4},{16,24},{20,28},{24,16},{28,20},{1,9},{5... | collective-permute-start | bytes 1572872 | tf_op jit(solution)/shard_map/ppermute | solution.py:148
  306.0 27.9 %collective-permute-start.20 = (bf16[512,512]{1,0:T(8,128)(2,1)}, bf16[512,512]{1,0:T(8,128)(2,1)}, u32[]{:S(2)}, u32[]{:S(2)}) collective-permute-start(bf16[512,512]{1,0:T(8,128)(2,1)} %select_convert_fusion.1), channel_id=1, source_target_pairs={{0,8},{4,12},{8,0},{12,4},{16,24},{20,28},{24,16},{28,20},{1,9},{5... | collective-permute-start | bytes 1572872 | tf_op jit(solution)/shard_map/ppermute | solution.py:148
  336.6 11.7 %collective-permute-start.21 = (bf16[512,512]{1,0:T(8,128)(2,1)}, bf16[512,512]{1,0:T(8,128)(2,1)}, u32[]{:S(2)}, u32[]{:S(2)}) collective-permute-start(bf16[512,512]{1,0:T(8,128)(2,1)} %get-tuple-element.33), channel_id=1, source_target_pairs={{0,16},{4,20},{8,24},{12,28},{16,0},{20,4},{24,8},{28,12},{1,17},{... | collective-permute-start | bytes 1572872 | tf_op jit(solution)/shard_map/ppermute | solution.py:148
  339.6 13.4 %collective-permute-start.18 = (bf16[512,512]{0,1:T(8,128)(2,1)}, bf16[512,512]{0,1:T(8,128)(2,1)}, u32[]{:S(2)}, u32[]{:S(2)}) collective-permute-start(bf16[512,512]{0,1:T(8,128)(2,1)} %get-tuple-element.45), channel_id=1, source_target_pairs={{0,8},{4,12},{8,0},{12,4},{16,24},{20,28},{24,16},{28,20},{1,9},{5... | collective-permute-start | bytes 1572872 | tf_op jit(solution)/shard_map/ppermute | solution.py:148
  357.7 63.2 %collective-permute-start.23 = (bf16[512,512]{0,1:T(8,128)(2,1)}, bf16[512,512]{0,1:T(8,128)(2,1)}, u32[]{:S(2)}, u32[]{:S(2)}) collective-permute-start(bf16[512,512]{0,1:T(8,128)(2,1)} %broadcast_select_fusion.10), channel_id=1, source_target_pairs={{1,12},{2,20},{3,28},{5,8},{6,16},{7,24},{8,5},{10,21},{11,29},{12... | collective-permute-start | bytes 1572872 | tf_op jit(solution)/shard_map/ppermute | solution.py:299
  363.2 68.9 %collective-permute-start.22 = (bf16[512,512]{0,1:T(8,128)(2,1)}, bf16[512,512]{0,1:T(8,128)(2,1)}, u32[]{:S(2)}, u32[]{:S(2)}) collective-permute-start(bf16[512,512]{0,1:T(8,128)(2,1)} %get-tuple-element.31), channel_id=1, source_target_pairs={{1,8},{2,16},{3,24},{5,12},{6,20},{7,28},{8,1},{10,17},{11,25},{12... | collective-permute-start | bytes 1572872 | tf_op jit(solution)/shard_map/ppermute | solution.py:298
  366.8 65.4 %copy-start.6 = (f32[512,512]{1,0:T(8,128)S(1)}, f32[512,512]{1,0:T(8,128)}, u32[]{:S(2)}) copy-start(f32[512,512]{1,0:T(8,128)} %convert_add_fusion) | copy-start | bytes 3145732
  (18 other events, 97.2 us)
